TPU v7x, 32 devices: a whole 2x2x4 slice. The times are simulated.
32 devices in a mesh: nodes: 16 (over z, y, x), heads: 2 (over core).
Axes of the slice: x: 2, y: 2, z: 4, core: 2. Of those that a mesh axis runs over, the one named last changes fastest.
Arguments:
- features: bfloat16 [12288, 512], P(('nodes', 'heads')), may hold values from -24 to 24
- w_qkv: bfloat16 [512, 3, 512], replicated, may hold values from -0.25 to 0.25
- w_out: bfloat16 [512, 512], replicated, may hold values from -0.25 to 0.25
- w_up: bfloat16 [512, 1024], replicated, may hold values from -0.25 to 0.25
- w_down: bfloat16 [1024, 512], replicated, may hold values from -0.1875 to 0.1875
- pattern: int32 [96, 128, 8], P(('nodes', 'heads')), may hold values from 0 to 65535
- partner: int32 [96, 4], P(('nodes', 'heads')), may hold values from 0 to 2, as said below
- counts: int32 [32], P(('nodes', 'heads')), may hold values from 1 to 3, as said below
Outputs:
- mixed: bfloat16 [12288, 512], P(('nodes', 'heads'))
Inputs may be any that keep to these rules, and one draw needn't show every extreme that they name: `partner`: each link of block slot s of device d names a live block slot of device d XOR 2**b_l; every live slot of that device is named by some slot of d. `counts`: some device holds 3 live blocks.
All inputs are finite; a program needn't handle non-finite values.
Results may differ from a plain program's by a relative error of at most 0.012.
The roundings to bfloat16 on the way count: a program that leaves them out, or rounds other values in their place, can miss the bound.
Values may be sent and summed in bfloat16 or wider, within the bound.
A program may use at most 64 MiB of HBM per device.

v0:
```python
import jax
import jax.numpy as jnp
from jax import lax
from jax.sharding import PartitionSpec as P

D = 512
H = 8


epsilon = 1e-05


def from_partner(value, axis, bit):
    mask = 2**bit
    pairs = [(source, source ^ mask) for source in range(lax.axis_size(axis))]
    return lax.ppermute(value, axis, pairs)


def unpack_bits(pattern_words, width):
    column = jnp.arange(width)
    picked = pattern_words[..., column // 16]
    bits = jnp.right_shift(picked, column % 16) & 1
    return (bits == 1) | jnp.eye(width, dtype=bool)


def local(features, w_qkv, w_out, w_up, w_down, pattern, partner, counts):
    row_count = features.shape[0]
    slot_count = partner.shape[0]
    block_rows = row_count // slot_count
    width = features.shape[1]
    head_size = D // H
    projected = jnp.einsum(
        "rd,dtc->rtc", features, w_qkv, preferred_element_type=jnp.float32
    ).astype(jnp.bfloat16)
    keys_values = projected[:, 1:, :]
    log_size = (lax.axis_size("nodes") * lax.axis_size("heads")).bit_length() - 1
    linked_parts = []
    for link_index in range(4):
        bit_place = link_index * log_size // 4
        if bit_place == 0:
            received = from_partner(keys_values, "heads", 0)
        else:
            received = from_partner(keys_values, "nodes", bit_place - 1)
        received = received.reshape(slot_count, block_rows, 2, width)
        linked_parts.append(jnp.take(received, partner[:, link_index], axis=0))
    own_blocks = projected.reshape(slot_count, block_rows, 3, width)
    all_keys = jnp.concatenate([own_blocks[:, :, 1:]] + linked_parts, axis=1)
    local_allowed = unpack_bits(pattern, block_rows)
    allowed = jnp.concatenate(
        [local_allowed, jnp.ones((slot_count, block_rows, 4 * block_rows), dtype=bool)], axis=2
    )
    score_scale = 1.0 / head_size**0.5
    head_outputs = []
    for head_index in range(H):
        lower = head_index * head_size
        queries = own_blocks[:, :, 0, lower : lower + head_size]
        keys = all_keys[:, :, 0, lower : lower + head_size]
        values = all_keys[:, :, 1, lower : lower + head_size]
        scores = (
            jnp.einsum("sqe,ske->sqk", queries, keys, preferred_element_type=jnp.float32)
            * score_scale
        )
        scores = jnp.where(allowed, scores, -1e30)
        top_score = jnp.max(scores, axis=-1, keepdims=True)
        expo = jnp.exp(scores - top_score)
        weights = (expo / jnp.sum(expo, axis=-1, keepdims=True)).astype(jnp.bfloat16)
        result = jnp.einsum("sqk,ske->sqe", weights, values, preferred_element_type=jnp.float32)
        head_outputs.append(result.astype(jnp.bfloat16))
    attended = jnp.concatenate(head_outputs, axis=-1).reshape(row_count, width)
    resid = features.astype(jnp.float32) + jnp.dot(
        attended, w_out, preferred_element_type=jnp.float32
    )
    row_mean = jnp.mean(resid, axis=1, keepdims=True)
    row_var = jnp.mean(resid * resid, axis=1, keepdims=True) - row_mean * row_mean
    normed = (resid - row_mean) * lax.rsqrt(row_var + epsilon)
    hidden = jax.nn.relu(
        jnp.dot(normed.astype(jnp.bfloat16), w_up, preferred_element_type=jnp.float32)
    ).astype(jnp.bfloat16)
    ffn = jnp.dot(hidden, w_down, preferred_element_type=jnp.float32)
    mixed = normed + ffn
    live_rows = jnp.arange(row_count) // block_rows < counts[0]
    return jnp.where(live_rows[:, None], mixed, 0.0).astype(jnp.bfloat16)


def solution(mesh):
    placed = (
        P(("nodes", "heads"), None),
        P(),
        P(),
        P(),
        P(),
        P(("nodes", "heads"), None, None),
        P(("nodes", "heads"), None),
        P(("nodes", "heads")),
    )
    return jax.shard_map(
        local, mesh=mesh, in_specs=placed, out_specs=P(("nodes", "heads"), None), check_vma=False
    )
```

profile of v0, /device:TPU:0, one launch (start us, length us, event | category | flops | bytes accessed | tf_op | source)
XLA Modules:
  0.0 110.1 jit_solution(637534503748713233)
XLA Ops:
  0.0 1.4 %copy-done = bf16[512,3,512]{2,0,1:T(8,128)(2,1)S(1)} copy-done((bf16[512,3,512]{2,0,1:T(8,128)(2,1)S(1)}, bf16[512,3,512]{2,0,1:T(8,128)(2,1)}, u32[]{:S(2)}) %copy-start) | copy-done | bytes 1572888
  1.4 1.8 %convolution_convert_fusion = bf16[384,3,512]{2,0,1:T(8,128)(2,1)S(1)} fusion(bf16[512,3,512]{2,0,1:T(8,128)(2,1)S(1)} %copy-done, bf16[384,512]{1,0:T(8,128)(2,1)} %param.10), kind=kOutput, calls=%fused_computation.22 | convolution fusion | flops 604569600 | bytes 3145728 | tf_op jit(solution)/shard_map/rd,dtc->rtc/dot_general | solution.py:32
  3.2 0.0 copy-start.4
  3.2 0.0 copy-start.1
  3.2 0.9 slice.132
  4.1 0.5 collective-permute-start
  4.6 2.5 %collective-permute-start.1 = (bf16[384,2,512]{2,0,1:T(8,128)(2,1)}, bf16[384,2,512]{2,0,1:T(8,128)(2,1)}, u32[]{:S(2)}, u32[]{:S(2)}) collective-permute-start(bf16[384,2,512]{2,0,1:T(8,128)(2,1)} %slice.132), channel_id=1, source_target_pairs={{0,2},{2,0},{4,6},{6,4},{8,10},{10,8},{12,14},{14,12},{16,18},{18,... | collective-permute-start | bytes 2359304 | tf_op jit(solution)/shard_map/ppermute | solution.py:16
  7.1 1.5 %collective-permute-start.2 = (bf16[384,2,512]{2,0,1:T(8,128)(2,1)}, bf16[384,2,512]{2,0,1:T(8,128)(2,1)}, u32[]{:S(2)}, u32[]{:S(2)}) collective-permute-start(bf16[384,2,512]{2,0,1:T(8,128)(2,1)} %slice.132), channel_id=1, source_target_pairs={{0,4},{2,6},{4,0},{6,2},{8,12},{10,14},{12,8},{14,10},{16,20},{18,... | collective-permute-start | bytes 2359304 | tf_op jit(solution)/shard_map/ppermute | solution.py:16
  8.6 1.6 %collective-permute-start.3 = (bf16[384,2,512]{2,0,1:T(8,128)(2,1)}, bf16[384,2,512]{2,0,1:T(8,128)(2,1)}, u32[]{:S(2)}, u32[]{:S(2)}) collective-permute-start(bf16[384,2,512]{2,0,1:T(8,128)(2,1)} %slice.132), channel_id=1, source_target_pairs={{0,8},{2,10},{4,12},{6,14},{8,0},{10,2},{12,4},{14,6},{16,24},{18,... | collective-permute-start | bytes 2359304 | tf_op jit(solution)/shard_map/ppermute | solution.py:16
  10.2 0.5 fusion.59
  10.7 0.6 iota_compare_fusion
  11.3 0.6 and_select_fusion
  11.9 1.0 slice.131
  12.9 1.5 %copy.38 = bf16[3,128,2,512]{1,3,0,2:T(8,128)(2,1)S(1)} copy(bf16[3,128,2,512]{3,1,0,2:T(8,128)(2,1)} %slice.131) | data formatting | bytes 1572864
  14.4 1.0 constant_dynamic-update-slice_fusion
  15.4 0.2 slice_reduce_fusion
  15.7 0.6 pad_clamp_fusion.4
  16.3 0.8 gather_fusion
  17.2 0.1 copy.18
  18.0 0.8 fusion.46
  18.8 2.2 %copy.21 = bf16[3,128,2,512]{3,1,2,0:T(8,128)(2,1)} copy(bf16[3,128,2,512]{3,1,0,2:T(8,128)(2,1)} %bitcast.6) | data formatting | bytes 1572864 | tf_op jit(solution)/shard_map/reshape | solution.py:44
  20.9 2.7 %gather_fusion.1 = bf16[3,128,2,512]{3,1,2,0:T(8,128)(2,1)} fusion(bf16[3,128,2,512]{3,1,2,0:T(8,128)(2,1)} %copy.21, s32[1024]{0:T(1024)S(1)} %pad_clamp_fusion.3), kind=kCustom, calls=%fused_computation.clone | custom fusion | bytes 1572876 | tf_op jit(solution)/shard_map/jit(_take)/gather | solution.py:45
  23.7 2.3 %copy.22 = bf16[3,128,2,512]{1,3,0,2:T(8,128)(2,1)} copy(bf16[3,128,2,512]{3,1,2,0:T(8,128)(2,1)} %gather_fusion.1) | data formatting | bytes 1572864 | tf_op jit(solution)/shard_map/jit(_take)/gather | solution.py:45
  26.0 2.2 %copy.23 = bf16[3,128,2,512]{3,1,2,0:T(8,128)(2,1)} copy(bf16[3,128,2,512]{3,1,0,2:T(8,128)(2,1)} %bitcast.7) | data formatting | bytes 1572864 | tf_op jit(solution)/shard_map/reshape | solution.py:44
  28.1 2.7 %gather_fusion.2 = bf16[3,128,2,512]{3,1,2,0:T(8,128)(2,1)} fusion(bf16[3,128,2,512]{3,1,2,0:T(8,128)(2,1)} %copy.23, s32[1024]{0:T(1024)S(1)} %pad_clamp_fusion.2), kind=kCustom, calls=%fused_computation.1.clone | custom fusion | bytes 1572876 | tf_op jit(solution)/shard_map/jit(_take)/gather | solution.py:45
  30.8 2.3 %copy.24 = bf16[3,128,2,512]{1,3,0,2:T(8,128)(2,1)} copy(bf16[3,128,2,512]{3,1,2,0:T(8,128)(2,1)} %gather_fusion.2) | data formatting | bytes 1572864 | tf_op jit(solution)/shard_map/jit(_take)/gather | solution.py:45
  33.1 2.2 %copy.25 = bf16[3,128,2,512]{3,1,2,0:T(8,128)(2,1)} copy(bf16[3,128,2,512]{3,1,0,2:T(8,128)(2,1)} %bitcast.8) | data formatting | bytes 1572864 | tf_op jit(solution)/shard_map/reshape | solution.py:44
  35.3 2.7 %gather_fusion.3 = bf16[3,128,2,512]{3,1,2,0:T(8,128)(2,1)} fusion(bf16[3,128,2,512]{3,1,2,0:T(8,128)(2,1)} %copy.25, s32[1024]{0:T(1024)S(1)} %pad_clamp_fusion.1), kind=kCustom, calls=%fused_computation.2.clone | custom fusion | bytes 1572876 | tf_op jit(solution)/shard_map/jit(_take)/gather | solution.py:45
  38.0 2.3 %copy.26 = bf16[3,128,2,512]{1,3,0,2:T(8,128)(2,1)} copy(bf16[3,128,2,512]{3,1,2,0:T(8,128)(2,1)} %gather_fusion.3) | data formatting | bytes 1572864 | tf_op jit(solution)/shard_map/jit(_take)/gather | solution.py:45
  40.3 2.1 %copy.27 = bf16[3,128,2,512]{3,1,2,0:T(8,128)(2,1)} copy(bf16[3,128,2,512]{3,1,0,2:T(8,128)(2,1)} %bitcast.9) | data formatting | bytes 1572864 | tf_op jit(solution)/shard_map/reshape | solution.py:44
  42.4 2.6 %gather_fusion.4 = bf16[3,128,2,512]{3,1,2,0:T(8,128)(2,1)} fusion(bf16[3,128,2,512]{3,1,2,0:T(8,128)(2,1)} %copy.27, s32[1024]{0:T(1024)S(1)} %pad_clamp_fusion), kind=kCustom, calls=%fused_computation.3.clone | custom fusion | bytes 1572876 | tf_op jit(solution)/shard_map/jit(_take)/gather | solution.py:45
  45.1 2.3 %copy.28 = bf16[3,128,2,512]{1,3,0,2:T(8,128)(2,1)} copy(bf16[3,128,2,512]{3,1,2,0:T(8,128)(2,1)} %gather_fusion.4) | data formatting | bytes 1572864 | tf_op jit(solution)/shard_map/jit(_take)/gather | solution.py:45
  47.4 2.4 %select_dynamic-update-slice_fusion.3 = bf16[3,640,2,512]{1,3,0,2:T(8,128)(2,1)} fusion(bf16[3,640,2,512]{1,3,0,2:T(8,128)(2,1)} %constant_dynamic-update-slice_fusion, bf16[3,128,2,512]{1,3,0,2:T(8,128)(2,1)} %copy.22, pred[3]{0:T(512)(128)(4,1)S(1)} %get-tuple-element.18), kind=kLoop, calls=%fused_computation.79 | loop fusion | flops 393216 | bytes 1572867
  49.8 2.4 %select_dynamic-update-slice_fusion.2 = bf16[3,640,2,512]{1,3,0,2:T(8,128)(2,1)} fusion(bf16[3,640,2,512]{1,3,0,2:T(8,128)(2,1)} %select_dynamic-update-slice_fusion.3, bf16[3,128,2,512]{1,3,0,2:T(8,128)(2,1)} %copy.24, pred[3]{0:T(512)(128)(4,1)S(1)} %get-tuple-element.17), kind=kLoop, calls=%fused_computation.78 | loop fusion | flops 393216 | bytes 1572867
  52.1 2.3 %select_dynamic-update-slice_fusion.1 = bf16[3,640,2,512]{1,3,0,2:T(8,128)(2,1)} fusion(bf16[3,640,2,512]{1,3,0,2:T(8,128)(2,1)} %select_dynamic-update-slice_fusion.2, bf16[3,128,2,512]{1,3,0,2:T(8,128)(2,1)} %copy.26, pred[3]{0:T(512)(128)(4,1)S(1)} %get-tuple-element.16), kind=kLoop, calls=%fused_computation.77 | loop fusion | flops 393216 | bytes 1572867
  54.4 1.2 %select_dynamic-update-slice_fusion = bf16[3,640,2,512]{1,3,0,2:T(8,128)(2,1)} fusion(bf16[3,640,2,512]{1,3,0,2:T(8,128)(2,1)} %select_dynamic-update-slice_fusion.1, bf16[3,128,2,512]{1,3,0,2:T(8,128)(2,1)S(1)} %copy-done.2, pred[3]{0:T(512)(128)(4,1)S(1)} %get-tuple-element.15), kind=kLoop, calls=%fused_computation.76 | loop fusion | flops 393216 | bytes 1572867 | tf_op jit(solution)/shard_map/concatenate | solution.py:47
  55.6 2.2 %pad_select_fusion.6 = f32[3,128,640]{2,1,0:T(8,128)} fusion(pred[3,128,128]{2,1,0:T(32,128)(4,1)S(1)} %fusion.46, bf16[3,640,2,512]{1,3,0,2:T(8,128)(2,1)} %select_dynamic-update-slice_fusion, bf16[3,128,3,512]{3,1,0,2:T(8,128)(2,1)S(1)} %bitcast.175), kind=kOutput, calls=%fused_computation.19 | convolution fusion | flops 31948800 | bytes 1376256 | tf_op jit(solution)/shard_map/sqe,ske->sqk/dot_general | solution.py:60
  57.8 1.5 %fusion.87 = f32[3,128]{1,0:T(4,128)S(1)} fusion(pred[3,128,128]{2,1,0:T(32,128)(4,1)S(1)} %fusion.46, bf16[3,640,2,512]{1,3,0,2:T(8,128)(2,1)} %select_dynamic-update-slice_fusion, bf16[3,128,3,512]{3,1,0,2:T(8,128)(2,1)S(1)} %bitcast.176), kind=kOutput, calls=%fused_computation.185 | convolution fusion | flops 32440960 | bytes 394752 | tf_op jit(solution)/shard_map/sub | solution.py:65
  59.3 2.2 %pad_select_fusion.7 = f32[3,128,640]{2,1,0:T(8,128)} fusion(pred[3,128,128]{2,1,0:T(32,128)(4,1)S(1)} %fusion.46, bf16[3,640,2,512]{1,3,0,2:T(8,128)(2,1)} %select_dynamic-update-slice_fusion, bf16[3,128,3,512]{3,1,0,2:T(8,128)(2,1)S(1)} %bitcast.177), kind=kOutput, calls=%fused_computation.20 | convolution fusion | flops 31948800 | bytes 1376256 | tf_op jit(solution)/shard_map/sqe,ske->sqk/dot_general | solution.py:60
  61.5 1.4 %fusion.86 = f32[3,128]{1,0:T(4,128)S(1)} fusion(pred[3,128,128]{2,1,0:T(32,128)(4,1)S(1)} %fusion.46, bf16[3,640,2,512]{1,3,0,2:T(8,128)(2,1)} %select_dynamic-update-slice_fusion, bf16[3,128,3,512]{3,1,0,2:T(8,128)(2,1)S(1)} %bitcast.178), kind=kOutput, calls=%fused_computation.184 | convolution fusion | flops 32440960 | bytes 394752 | tf_op jit(solution)/shard_map/sub | solution.py:65
  62.9 2.2 %pad_select_fusion.5 = f32[3,128,640]{2,1,0:T(8,128)} fusion(pred[3,128,128]{2,1,0:T(32,128)(4,1)S(1)} %fusion.46, bf16[3,640,2,512]{1,3,0,2:T(8,128)(2,1)} %select_dynamic-update-slice_fusion, bf16[3,128,3,512]{3,1,0,2:T(8,128)(2,1)S(1)} %bitcast.179), kind=kOutput, calls=%fused_computation.18 | convolution fusion | flops 31948800 | bytes 1376256 | tf_op jit(solution)/shard_map/sqe,ske->sqk/dot_general | solution.py:60
  65.1 1.4 %fusion.88 = f32[3,128]{1,0:T(4,128)S(1)} fusion(pred[3,128,128]{2,1,0:T(32,128)(4,1)S(1)} %fusion.46, bf16[3,640,2,512]{1,3,0,2:T(8,128)(2,1)} %select_dynamic-update-slice_fusion, bf16[3,128,3,512]{3,1,0,2:T(8,128)(2,1)S(1)} %bitcast.180), kind=kOutput, calls=%fused_computation.186 | convolution fusion | flops 32440960 | bytes 394752 | tf_op jit(solution)/shard_map/sub | solution.py:65
  66.6 2.2 %pad_select_fusion.4 = f32[3,128,640]{2,1,0:T(8,128)} fusion(pred[3,128,128]{2,1,0:T(32,128)(4,1)S(1)} %fusion.46, bf16[3,640,2,512]{1,3,0,2:T(8,128)(2,1)} %select_dynamic-update-slice_fusion, bf16[3,128,3,512]{3,1,0,2:T(8,128)(2,1)S(1)} %bitcast.181), kind=kOutput, calls=%fused_computation.17 | convolution fusion | flops 31948800 | bytes 1376256 | tf_op jit(solution)/shard_map/sqe,ske->sqk/dot_general | solution.py:60
  68.8 1.5 %fusion.89 = f32[3,128]{1,0:T(4,128)S(1)} fusion(pred[3,128,128]{2,1,0:T(32,128)(4,1)S(1)} %fusion.46, bf16[3,640,2,512]{1,3,0,2:T(8,128)(2,1)} %select_dynamic-update-slice_fusion, bf16[3,128,3,512]{3,1,0,2:T(8,128)(2,1)S(1)} %bitcast.182), kind=kOutput, calls=%fused_computation.187 | convolution fusion | flops 32440960 | bytes 394752 | tf_op jit(solution)/shard_map/sub | solution.py:65
  70.3 2.3 %pad_select_fusion.3 = f32[3,128,640]{2,1,0:T(8,128)} fusion(pred[3,128,128]{2,1,0:T(32,128)(4,1)S(1)} %fusion.46, bf16[3,640,2,512]{1,3,0,2:T(8,128)(2,1)} %select_dynamic-update-slice_fusion, bf16[3,128,3,512]{3,1,0,2:T(8,128)(2,1)S(1)} %bitcast.183), kind=kOutput, calls=%fused_computation.16 | convolution fusion | flops 31948800 | bytes 1376256 | tf_op jit(solution)/shard_map/sqe,ske->sqk/dot_general | solution.py:60
  72.6 1.4 %fusion.90 = f32[3,128]{1,0:T(4,128)S(1)} fusion(pred[3,128,128]{2,1,0:T(32,128)(4,1)S(1)} %fusion.46, bf16[3,640,2,512]{1,3,0,2:T(8,128)(2,1)} %select_dynamic-update-slice_fusion, bf16[3,128,3,512]{3,1,0,2:T(8,128)(2,1)S(1)} %bitcast.184), kind=kOutput, calls=%fused_computation.188 | convolution fusion | flops 32440960 | bytes 394752 | tf_op jit(solution)/shard_map/sub | solution.py:65
  74.0 2.3 %pad_select_fusion.2 = f32[3,128,640]{2,1,0:T(8,128)} fusion(pred[3,128,128]{2,1,0:T(32,128)(4,1)S(1)} %fusion.46, bf16[3,640,2,512]{1,3,0,2:T(8,128)(2,1)} %select_dynamic-update-slice_fusion, bf16[3,128,3,512]{3,1,0,2:T(8,128)(2,1)S(1)} %bitcast.185), kind=kOutput, calls=%fused_computation.15 | convolution fusion | flops 31948800 | bytes 1376256 | tf_op jit(solution)/shard_map/sqe,ske->sqk/dot_general | solution.py:60
  76.3 1.5 %fusion.91 = f32[3,128]{1,0:T(4,128)S(1)} fusion(pred[3,128,128]{2,1,0:T(32,128)(4,1)S(1)} %fusion.46, bf16[3,640,2,512]{1,3,0,2:T(8,128)(2,1)} %select_dynamic-update-slice_fusion, bf16[3,128,3,512]{3,1,0,2:T(8,128)(2,1)S(1)} %bitcast.186), kind=kOutput, calls=%fused_computation.189 | convolution fusion | flops 32440960 | bytes 394752 | tf_op jit(solution)/shard_map/sub | solution.py:65
  77.8 2.2 %pad_select_fusion.1 = f32[3,128,640]{2,1,0:T(8,128)} fusion(pred[3,128,128]{2,1,0:T(32,128)(4,1)S(1)} %fusion.46, bf16[3,640,2,512]{1,3,0,2:T(8,128)(2,1)} %select_dynamic-update-slice_fusion, bf16[3,128,3,512]{3,1,0,2:T(8,128)(2,1)S(1)} %bitcast.187), kind=kOutput, calls=%fused_computation.14 | convolution fusion | flops 31948800 | bytes 1376256 | tf_op jit(solution)/shard_map/sqe,ske->sqk/dot_general | solution.py:60
  80.0 1.4 %fusion.92 = f32[3,128]{1,0:T(4,128)S(1)} fusion(pred[3,128,128]{2,1,0:T(32,128)(4,1)S(1)} %fusion.46, bf16[3,640,2,512]{1,3,0,2:T(8,128)(2,1)} %select_dynamic-update-slice_fusion, bf16[3,128,3,512]{3,1,0,2:T(8,128)(2,1)S(1)} %bitcast.188), kind=kOutput, calls=%fused_computation.190 | convolution fusion | flops 32440960 | bytes 394752 | tf_op jit(solution)/shard_map/sub | solution.py:65
  81.5 2.3 %pad_select_fusion = f32[3,128,640]{2,1,0:T(8,128)} fusion(pred[3,128,128]{2,1,0:T(32,128)(4,1)S(1)} %fusion.46, bf16[3,640,2,512]{1,3,0,2:T(8,128)(2,1)} %select_dynamic-update-slice_fusion, bf16[3,128,3,512]{3,1,0,2:T(8,128)(2,1)S(1)} %bitcast.189), kind=kOutput, calls=%fused_computation.13 | convolution fusion | flops 31948800 | bytes 1376256 | tf_op jit(solution)/shard_map/sqe,ske->sqk/dot_general | solution.py:60
  83.7 1.5 %fusion.93 = f32[3,128]{1,0:T(4,128)S(1)} fusion(pred[3,128,128]{2,1,0:T(32,128)(4,1)S(1)} %fusion.46, bf16[3,640,2,512]{1,3,0,2:T(8,128)(2,1)} %select_dynamic-update-slice_fusion, bf16[3,128,3,512]{3,1,0,2:T(8,128)(2,1)S(1)} %bitcast.190), kind=kOutput, calls=%fused_computation.191 | convolution fusion | flops 32440960 | bytes 394752 | tf_op jit(solution)/shard_map/sub | solution.py:65
  85.2 2.4 %fusion.35 = bf16[3,128,512]{1,2,0:T(8,128)(2,1)S(1)} fusion(f32[3,128]{1,0:T(4,128)S(1)} %fusion.86, bf16[3,640,2,512]{1,3,0,2:T(8,128)(2,1)} %select_dynamic-update-slice_fusion, f32[3,128,640]{2,1,0:T(8,128)} %pad_select_fusion.7), kind=kOutput, calls=%fused_computation.67 | convolution fusion | flops 32220158 | bytes 2262528 | tf_op jit(solution)/shard_map/sqk,ske->sqe/dot_general | solution.py:67
  87.6 2.4 %fusion.34 = bf16[3,128,512]{1,2,0:T(8,128)(2,1)S(1)} fusion(bf16[3,128,512]{1,2,0:T(8,128)(2,1)S(1)} %fusion.35, f32[3,128]{1,0:T(4,128)S(1)} %fusion.87, bf16[3,640,2,512]{1,3,0,2:T(8,128)(2,1)} %select_dynamic-update-slice_fusion, f32[3,128,640]{2,1,0:T(8,128)} %pad_select_fusion.6), kind=kOutput, calls=%fused_computation.65 | convolution fusion | flops 32220160 | bytes 2263040 | tf_op jit(solution)/shard_map/sqk,ske->sqe/dot_general | solution.py:67
  90.1 2.4 %fusion.33 = bf16[3,128,512]{1,2,0:T(8,128)(2,1)S(1)} fusion(bf16[3,128,512]{1,2,0:T(8,128)(2,1)S(1)} %fusion.34, f32[3,128]{1,0:T(4,128)S(1)} %fusion.88, bf16[3,640,2,512]{1,3,0,2:T(8,128)(2,1)} %select_dynamic-update-slice_fusion, f32[3,128,640]{2,1,0:T(8,128)} %pad_select_fusion.5), kind=kOutput, calls=%fused_computation.63 | convolution fusion | flops 32220160 | bytes 2263040 | tf_op jit(solution)/shard_map/sqk,ske->sqe/dot_general | solution.py:67
  92.5 2.4 %fusion.32 = bf16[3,128,512]{1,2,0:T(8,128)(2,1)S(1)} fusion(bf16[3,128,512]{1,2,0:T(8,128)(2,1)S(1)} %fusion.33, f32[3,128]{1,0:T(4,128)S(1)} %fusion.89, bf16[3,640,2,512]{1,3,0,2:T(8,128)(2,1)} %select_dynamic-update-slice_fusion, f32[3,128,640]{2,1,0:T(8,128)} %pad_select_fusion.4), kind=kOutput, calls=%fused_computation.61 | convolution fusion | flops 32220160 | bytes 2263040 | tf_op jit(solution)/shard_map/sqk,ske->sqe/dot_general | solution.py:67
  94.9 2.7 %fusion.31 = bf16[3,128,512]{1,2,0:T(8,128)(2,1)S(1)} fusion(bf16[3,128,512]{1,2,0:T(8,128)(2,1)S(1)} %fusion.32, f32[3,128]{1,0:T(4,128)S(1)} %fusion.90, bf16[3,640,2,512]{1,3,0,2:T(8,128)(2,1)} %select_dynamic-update-slice_fusion, f32[3,128,640]{2,1,0:T(8,128)} %pad_select_fusion.3), kind=kOutput, calls=%fused_computation.59 | convolution fusion | flops 32220160 | bytes 2263040 | tf_op jit(solution)/shard_map/sqk,ske->sqe/dot_general | solution.py:67
  97.7 2.5 %fusion.30 = bf16[3,128,512]{1,2,0:T(8,128)(2,1)S(1)} fusion(bf16[3,128,512]{1,2,0:T(8,128)(2,1)S(1)} %fusion.31, f32[3,128]{1,0:T(4,128)S(1)} %fusion.91, bf16[3,640,2,512]{1,3,0,2:T(8,128)(2,1)} %select_dynamic-update-slice_fusion, f32[3,128,640]{2,1,0:T(8,128)} %pad_select_fusion.2), kind=kOutput, calls=%fused_computation.57 | convolution fusion | flops 32220160 | bytes 2263040 | tf_op jit(solution)/shard_map/sqk,ske->sqe/dot_general | solution.py:67
  100.2 0.0 copy-start.3
  100.2 2.4 %fusion.29 = bf16[3,128,512]{1,2,0:T(8,128)(2,1)S(1)} fusion(bf16[3,128,512]{1,2,0:T(8,128)(2,1)S(1)} %fusion.30, f32[3,128]{1,0:T(4,128)S(1)} %fusion.92, bf16[3,640,2,512]{1,3,0,2:T(8,128)(2,1)} %select_dynamic-update-slice_fusion, f32[3,128,640]{2,1,0:T(8,128)} %pad_select_fusion.1), kind=kOutput, calls=%fused_computation.55 | convolution fusion | flops 32220160 | bytes 2263040 | tf_op jit(solution)/shard_map/sqk,ske->sqe/dot_general | solution.py:67
  102.6 2.4 %fusion.28 = bf16[3,128,512]{1,2,0:T(8,128)(2,1)S(1)} fusion(bf16[3,128,512]{1,2,0:T(8,128)(2,1)S(1)} %fusion.29, f32[3,128]{1,0:T(4,128)S(1)} %fusion.93, bf16[3,640,2,512]{1,3,0,2:T(8,128)(2,1)} %select_dynamic-update-slice_fusion, f32[3,128,640]{2,1,0:T(8,128)} %pad_select_fusion), kind=kOutput, calls=%fused_computation.53 | convolution fusion | flops 32220160 | bytes 2263040 | tf_op jit(solution)/shard_map/sqk,ske->sqe/dot_general | solution.py:67
  105.0 0.2 copy.36
  105.2 1.5 %fusion.85 = (f32[384]{0:T(512)S(1)}, f32[384]{0:T(512)S(1)}, f32[384,512]{1,0:T(8,128)S(1)}) fusion(bf16[384,512]{1,0:T(8,128)(2,1)S(1)} %bitcast.191, bf16[512,512]{1,0:T(8,128)(2,1)S(1)} %copy-done.3, bf16[384,512]{1,0:T(8,128)(2,1)} %param.10), kind=kOutput, calls=%fused_computation.183 | convolution fusion | flops 202308864 | bytes 2100224 | tf_op jit(solution)/shard_map/dot_general | solution.py:70
  106.8 3.3 %fusion.27 = bf16[384,512]{1,0:T(8,128)(2,1)} fusion(bf16[1024,512]{1,0:T(8,128)(2,1)} %param.14, bf16[512,1024]{1,0:T(8,128)(2,1)} %param.13, f32[384,512]{1,0:T(8,128)S(1)} %get-tuple-element.14, f32[384]{0:T(512)S(1)} %get-tuple-element.13, f32[384]{0:T(512)S(1)} %get-tuple-element.12, pred[384]{0:T(512)(128)(4,1)S(1)} %fusion.55), kind=kOutput, calls=%fused_computation.51 | convolution fusion | flops 807665664 | bytes 3280256 | tf_op jit(solution)/shard_map/dot_general | solution.py:79
  (22 shorter events, 0.1 us)
Async XLA Ops:
  0.0 1.4 %copy-start = (bf16[512,3,512]{2,0,1:T(8,128)(2,1)S(1)}, bf16[512,3,512]{2,0,1:T(8,128)(2,1)}, u32[]{:S(2)}) copy-start(bf16[512,3,512]{2,0,1:T(8,128)(2,1)} %param.11) | copy-start | bytes 4718596
  3.2 12.2 %copy-start.4 = (s32[3,4]{1,0:T(4,128)S(1)}, s32[3,4]{1,0:T(4,128)}, u32[]{:S(2)}) copy-start(s32[3,4]{1,0:T(4,128)} %param.16) | copy-start | bytes 148
  3.2 13.1 %copy-start.1 = (s32[3,128,8]{1,2,0:T(8,128)S(1)}, s32[3,128,8]{1,2,0:T(8,128)}, u32[]{:S(2)}) copy-start(s32[3,128,8]{1,2,0:T(8,128)} %param.15) | copy-start | bytes 36868
  4.1 14.6 %collective-permute-start = (bf16[384,2,512]{2,0,1:T(8,128)(2,1)}, bf16[384,2,512]{2,0,1:T(8,128)(2,1)}, u32[]{:S(2)}, u32[]{:S(2)}) collective-permute-start(bf16[384,2,512]{2,0,1:T(8,128)(2,1)} %slice.132), channel_id=1, source_target_pairs={{0,1},{1,0},{2,3},{3,2},{4,5},{5,4},{6,7},{7,6},{8,9},{9,8},{10,11... | collective-permute-start | bytes 2359304 | tf_op jit(solution)/shard_map/ppermute | solution.py:16
  4.6 21.4 %collective-permute-start.1 = (bf16[384,2,512]{2,0,1:T(8,128)(2,1)}, bf16[384,2,512]{2,0,1:T(8,128)(2,1)}, u32[]{:S(2)}, u32[]{:S(2)}) collective-permute-start(bf16[384,2,512]{2,0,1:T(8,128)(2,1)} %slice.132), channel_id=1, source_target_pairs={{0,2},{2,0},{4,6},{6,4},{8,10},{10,8},{12,14},{14,12},{16,18},{18,... | collective-permute-start | bytes 2359304 | tf_op jit(solution)/shard_map/ppermute | solution.py:16
  7.1 26.0 %collective-permute-start.2 = (bf16[384,2,512]{2,0,1:T(8,128)(2,1)}, bf16[384,2,512]{2,0,1:T(8,128)(2,1)}, u32[]{:S(2)}, u32[]{:S(2)}) collective-permute-start(bf16[384,2,512]{2,0,1:T(8,128)(2,1)} %slice.132), channel_id=1, source_target_pairs={{0,4},{2,6},{4,0},{6,2},{8,12},{10,14},{12,8},{14,10},{16,20},{18,... | collective-permute-start | bytes 2359304 | tf_op jit(solution)/shard_map/ppermute | solution.py:16
  8.6 31.7 %collective-permute-start.3 = (bf16[384,2,512]{2,0,1:T(8,128)(2,1)}, bf16[384,2,512]{2,0,1:T(8,128)(2,1)}, u32[]{:S(2)}, u32[]{:S(2)}) collective-permute-start(bf16[384,2,512]{2,0,1:T(8,128)(2,1)} %slice.132), channel_id=1, source_target_pairs={{0,8},{2,10},{4,12},{6,14},{8,0},{10,2},{12,4},{14,6},{16,24},{18,... | collective-permute-start | bytes 2359304 | tf_op jit(solution)/shard_map/ppermute | solution.py:16
  47.4 7.0 %copy-start.2 = (bf16[3,128,2,512]{1,3,0,2:T(8,128)(2,1)S(1)}, bf16[3,128,2,512]{1,3,0,2:T(8,128)(2,1)}, u32[]{:S(2)}) copy-start(bf16[3,128,2,512]{1,3,0,2:T(8,128)(2,1)} %copy.28) | copy-start | bytes 2359300
  100.2 5.0 %copy-start.3 = (bf16[512,512]{1,0:T(8,128)(2,1)S(1)}, bf16[512,512]{1,0:T(8,128)(2,1)}, u32[]{:S(2)}) copy-start(bf16[512,512]{1,0:T(8,128)(2,1)} %param.12) | copy-start | bytes 1572868
where the time goes:
time: 112 us; the launch traced here: 110 us
  matrix products  56 us (50%)
  local copies, waits for them, and re-layouts  35.8 us (32%)
  other arithmetic  11.4 us (10%)
  starting transfers between devices  6.04 us (5%)
    gather x8, local copies, waits for them, and re-layouts, local(): linked_parts.append(jnp.take(received, partner[:, link_index], axis=0))  20 us
    dot_general x8, matrix products, local(): jnp.einsum('sqk,ske->sqe', weights, values, preferred_element_type=jnp.fl...  19.8 us
    dot_general x8, matrix products, local(): jnp.einsum('sqe,ske->sqk', queries, keys, preferred_element_type=jnp.floa...  17.9 us
    sub x8, matrix products, local(): expo = jnp.exp(scores - top_score)  11.8 us
    reshape x4, local copies, waits for them, and re-layouts, local(): received = received.reshape(slot_count, block_rows, 2, width)  8.56 us
    unnamed x3, other arithmetic  7.02 us
    ppermute x4, starting transfers between devices, from_partner(): return lax.ppermute(value, axis, pairs)  6.04 us
    unnamed x12, local copies, waits for them, and re-layouts  3.91 us
  transfers between devices with their start and end apart: 4, of which 0 were waited for; matrix products, arithmetic and copies ran while one was open for 27% of the time, Pallas kernels for 0%

commit v1 on v0

v1 whole, which is shorter than its diff:
```python
import functools

import jax
import jax.numpy as jnp
from jax import lax
from jax.experimental import pallas as pl
from jax.experimental.pallas import tpu as pltpu
from jax.sharding import PartitionSpec as P

D = 512
H = 8
HD = D // H
PAIRS = H // 2
LINKS = 4

epsilon = 1e-05
F32 = jnp.float32
BF16 = jnp.bfloat16


def flip(index, mask):
    return index + mask - 2 * mask * ((index // mask) % 2)


def dot_nn(a, b):
    return jnp.dot(a, b, preferred_element_type=F32)


def dot_nt(a, b):
    return lax.dot_general(a, b, (((1,), (1,)), ((), ())), preferred_element_type=F32)


def kernel(
    bits, slots, blk,
    feat_hbm, w3_hbm, wo_hbm, wu_hbm, wd_hbm, pat_hbm, partner, counts,
    out_ref,
    x, w3, wo, wu, wd, pat, wqt, wvt, near, far,
    qpad, kown, vown, knear, vnear, kfar, vfar,
    ob, mb, lb, of, mf, lf, att,
    load_sem, near_send, near_recv, far_send, far_recv,
):
    node = lax.axis_index("nodes")
    core = lax.axis_index("heads")

    def target(bit):
        if bit == 0:
            return (node, flip(core, 1))
        return (flip(node, 2 ** (bit - 1)), core)

    loads = []
    for i, (src, dst) in enumerate(
        [(w3_hbm, w3), (feat_hbm, x), (pat_hbm, pat), (wo_hbm, wo), (wu_hbm, wu), (wd_hbm, wd)]
    ):
        loads.append(pltpu.make_async_copy(src, dst, load_sem.at[i]))
        loads[-1].start()

    barrier = pltpu.get_barrier_semaphore()
    for bit in bits:
        pl.semaphore_signal(
            barrier, inc=1, device_id=target(bit), device_id_type=pl.DeviceIdType.MESH
        )
    pl.semaphore_wait(barrier, LINKS)

    far_copies = []
    near_copy = pltpu.make_async_remote_copy(
        src_ref=feat_hbm, dst_ref=near, send_sem=near_send, recv_sem=near_recv,
        device_id=target(bits[0]), device_id_type=pl.DeviceIdType.MESH,
    )
    for j in range(slots):
        row = []
        for l in range(LINKS - 1):
            row.append(pltpu.make_async_remote_copy(
                src_ref=feat_hbm.at[pl.ds(j * blk, blk)],
                dst_ref=far.at[j, pl.ds(l * blk, blk)],
                send_sem=far_send.at[j, l], recv_sem=far_recv.at[j, l],
                device_id=target(bits[l + 1]), device_id_type=pl.DeviceIdType.MESH,
            ))
            row[-1].start()
        far_copies.append(row)
        if j == 0:
            near_copy.start()

    loads[0].wait()
    loads[1].wait()
    wqt[...] = w3[0].T
    wvt[...] = w3[2].T
    own = x[...]
    qt = dot_nt(wqt[...], own).astype(BF16) * jnp.asarray(1.0 / HD**0.5, BF16)
    zero = jnp.zeros((HD, blk), BF16)
    for s in range(slots):
        for p in range(PAIRS):
            a = qt[2 * p * HD : (2 * p + 1) * HD, s * blk : (s + 1) * blk]
            b = qt[(2 * p + 1) * HD : (2 * p + 2) * HD, s * blk : (s + 1) * blk]
            qpad[s, p] = jnp.concatenate(
                [jnp.concatenate([a, zero], 1), jnp.concatenate([zero, b], 1)], 0
            )

    def project(rows, put_k, put_v):
        k = dot_nn(rows, w3[1]).astype(BF16)
        v = dot_nt(wvt[...], rows).astype(BF16)
        for i in range(slots):
            put_k(i, k[i * blk : (i + 1) * blk])
            put_v(i, v[:, i * blk : (i + 1) * blk])

    def setter(ref, where):
        def put(i, value):
            ref[where(i)] = value
        return put

    project(own, setter(kown, lambda i: i), setter(vown, lambda i: i))
    near_copy.wait_recv()
    project(near[...], setter(knear, lambda i: i), setter(vnear, lambda i: i))
    loads[2].wait()

    def keep(o, m, l, o_ref, m_ref, l_ref, at, p):
        o_ref[at + (pl.ds(2 * p * HD, HD),)] = o[:HD, :blk]
        o_ref[at + (pl.ds((2 * p + 1) * HD, HD),)] = o[HD:, blk:]
        for half in range(2):
            cols = slice(half * blk, (half + 1) * blk)
            m_ref[at + (pl.ds(2 * p + half, 1),)] = m[:, cols]
            l_ref[at + (pl.ds(2 * p + half, 1),)] = l[:, cols]

    bit_row = lax.broadcasted_iota(jnp.int32, (16, blk), 0)
    key_at = lax.broadcasted_iota(jnp.int32, (blk, blk), 0)
    query_at = lax.broadcasted_iota(jnp.int32, (blk, blk), 1)
    for s in range(slots):
        words = pat[s]
        picked = jnp.concatenate(
            [
                jnp.right_shift(jnp.broadcast_to(words[w : w + 1], (16, blk)), bit_row) & 1
                for w in range(blk // 16)
            ],
            0,
        )
        bias = jnp.where((picked == 1) | (key_at == query_at), 0.0, -1e30).astype(F32)
        bias = jnp.concatenate([bias, bias], 1)
        linked = partner[s, 0]
        k1 = knear[linked]
        v1 = vnear[linked]
        for p in range(PAIRS):
            cols = slice(2 * p * HD, 2 * (p + 1) * HD)
            q = qpad[s, p]
            s0 = dot_nn(kown[s, :, cols], q) + bias
            s1 = dot_nn(k1[:, cols], q)
            m = jnp.maximum(jnp.max(s0, 0, keepdims=True), jnp.max(s1, 0, keepdims=True))
            e0 = jnp.exp(s0 - m)
            e1 = jnp.exp(s1 - m)
            l = jnp.sum(e0, 0, keepdims=True) + jnp.sum(e1, 0, keepdims=True)
            o = dot_nn(
                jnp.concatenate([vown[s, cols], v1[cols]], 1),
                jnp.concatenate([e0.astype(BF16), e1.astype(BF16)], 0),
            )
            keep(o, m, l, ob, mb, lb, (s,), p)

    ranks, order = [], []
    for l in range(1, LINKS):
        named = [partner[s, l] for s in range(slots)]
        rank = []
        for s in range(slots):
            r = jnp.int32(0)
            for t in range(slots):
                if t != s:
                    before = named[t] <= named[s] if t < s else named[t] < named[s]
                    r = r + jnp.where(before, 1, 0).astype(jnp.int32)
            rank.append(r)
        at = []
        for j in range(slots):
            slot, block = jnp.int32(0), jnp.int32(0)
            for s in range(slots):
                slot = jnp.where(rank[s] == j, s, slot)
                block = jnp.where(rank[s] == j, named[s], block)
            at.append((slot, block))
        ranks.append(rank)
        order.append(at)

    for j in range(slots):
        for l in range(LINKS - 1):
            far_copies[j][l].wait_recv()
        rows = far[j]
        k = dot_nn(rows, w3[1]).astype(BF16)
        v = dot_nt(wvt[...], rows).astype(BF16)
        for l in range(LINKS - 1):
            kfar[l, j] = k[l * blk : (l + 1) * blk]
            vfar[l, j] = v[:, l * blk : (l + 1) * blk]
        for l in range(LINKS - 1):
            slot, block = order[l][j]
            kj = kfar[l, block]
            vj = vfar[l, block]
            for p in range(PAIRS):
                cols = slice(2 * p * HD, 2 * (p + 1) * HD)
                scores = dot_nn(kj[:, cols], qpad[slot, p])
                m = jnp.max(scores, 0, keepdims=True)
                e = jnp.exp(scores - m)
                o = dot_nn(vj[cols], e.astype(BF16))
                keep(o, m, jnp.sum(e, 0, keepdims=True), of, mf, lf, (l, j), p)

    for s in range(slots):
        ms = [mb[s]] + [mf[l, ranks[l][s]] for l in range(LINKS - 1)]
        ls = [lb[s]] + [lf[l, ranks[l][s]] for l in range(LINKS - 1)]
        os = [ob[s]] + [of[l, ranks[l][s]] for l in range(LINKS - 1)]
        top = functools.reduce(jnp.maximum, ms)
        scale = [jnp.exp(m - top) for m in ms]
        total = functools.reduce(jnp.add, [a * b for a, b in zip(scale, ls)])
        scale = [a / total for a in scale]
        heads = []
        for h in range(H):
            heads.append(functools.reduce(
                jnp.add,
                [o[h * HD : (h + 1) * HD] * a[h : h + 1] for o, a in zip(os, scale)],
            ))
        joined = jnp.concatenate(heads, 0)
        att[pl.ds(s * blk, blk)] = joined.T.astype(BF16)

    for i in (3, 4, 5):
        loads[i].wait()
    resid = x[...].astype(F32) + dot_nn(att[...], wo[...])
    mean = jnp.mean(resid, 1, keepdims=True)
    var = jnp.mean(resid * resid, 1, keepdims=True) - mean * mean
    normed = (resid - mean) * lax.rsqrt(var + epsilon)
    hidden = jnp.maximum(dot_nn(normed.astype(BF16), wu[...]), 0.0).astype(BF16)
    mixed = normed + dot_nn(hidden, wd[...])
    live = counts[0]
    for s in range(slots):
        part = mixed[s * blk : (s + 1) * blk]
        out_ref[pl.ds(s * blk, blk)] = jnp.where(s < live, part, 0.0).astype(BF16)

    near_copy.wait_send()
    for row in far_copies:
        for copy in row:
            copy.wait_send()


def local(features, w_qkv, w_out, w_up, w_down, pattern, partner, counts):
    rows, width = features.shape
    slots = partner.shape[0]
    blk = rows // slots
    ff = w_up.shape[1]
    words = pattern.shape[2]
    log_size = (lax.axis_size("nodes") * lax.axis_size("heads")).bit_length() - 1
    bits = [i * log_size // 4 for i in range(LINKS)]
    far = LINKS - 1
    any_spec = pl.BlockSpec(memory_space=pl.ANY)
    smem = pl.BlockSpec(memory_space=pltpu.SMEM)
    vm = pltpu.VMEM
    sem = pltpu.SemaphoreType.DMA
    return pl.pallas_call(
        functools.partial(kernel, bits, slots, blk),
        out_shape=jax.ShapeDtypeStruct((rows, width), BF16),
        in_specs=[any_spec] * 6 + [smem] * 2,
        out_specs=pl.BlockSpec(memory_space=pltpu.VMEM),
        scratch_shapes=[
            vm((rows, width), BF16),
            vm((3, width, width), BF16),
            vm((width, width), BF16),
            vm((width, ff), BF16),
            vm((ff, width), BF16),
            vm((slots, words, blk), jnp.int32),
            vm((width, width), BF16),
            vm((width, width), BF16),
            vm((rows, width), BF16),
            vm((slots, far * blk, width), BF16),
            vm((slots, PAIRS, 2 * HD, 2 * blk), BF16),
            vm((slots, blk, width), BF16),
            vm((slots, width, blk), BF16),
            vm((slots, blk, width), BF16),
            vm((slots, width, blk), BF16),
            vm((far, slots, blk, width), BF16),
            vm((far, slots, width, blk), BF16),
            vm((slots, width, blk), F32),
            vm((slots, H, blk), F32),
            vm((slots, H, blk), F32),
            vm((far, slots, width, blk), F32),
            vm((far, slots, H, blk), F32),
            vm((far, slots, H, blk), F32),
            vm((rows, width), BF16),
            sem((6,)),
            sem,
            sem,
            sem((slots, far)),
            sem((slots, far)),
        ],
        compiler_params=pltpu.CompilerParams(
            collective_id=0, has_side_effects=True, vmem_limit_bytes=60 * 2**20
        ),
        cost_estimate=pl.CostEstimate(
            flops=5 * 10**9, bytes_accessed=10 * 2**20, transcendentals=2 * 10**6
        ),
        name="layer",
    )(
        features, jnp.transpose(w_qkv, (1, 0, 2)), w_out, w_up, w_down,
        jnp.transpose(pattern, (0, 2, 1)), partner, counts,
    )


def solution(mesh):
    placed = (
        P(("nodes", "heads"), None),
        P(),
        P(),
        P(),
        P(),
        P(("nodes", "heads"), None, None),
        P(("nodes", "heads"), None),
        P(("nodes", "heads")),
    )
    return jax.shard_map(
        local, mesh=mesh, in_specs=placed, out_specs=P(("nodes", "heads"), None), check_vma=False
    )
```

time: 112 us -> 20.9 us (0.19); the launches traced: 110 us -> 20.8 us
  matrix products: 56 us -> 0 us
  local copies, waits for them, and re-layouts: 35.8 us -> 1.77 us
  Pallas kernels: 0 us -> 18.3 us
  other arithmetic: 11.4 us -> 0 us
  starting transfers between devices: 6.04 us -> 0 us
    dot_general x19 -> x0, matrix products: 44.2 us -> none  [the longest x8 19.8 us: local(): jnp.einsum('sqk,ske->sqe', weights, values, preferred_element_type=jnp.fl...]
    gather x10 -> x0, local copies, waits for them, and re-layouts: 21 us -> none  [the longest x8 20 us: local(): linked_parts.append(jnp.take(received, partner[:, link_index], axis=0))]
    pallas_call x0 -> x1, Pallas kernels: none -> 18.3 us  [local(): pl.pallas_call(functools.partial(kernel, bits, slots, blk), out_shape=jax...]
    sub x8 -> x0, matrix products: 11.8 us -> none  [local(): expo = jnp.exp(scores - top_score)]
    reshape x4 -> x0, local copies, waits for them, and re-layouts: 8.56 us -> none  [local(): received = received.reshape(slot_count, block_rows, 2, width)]
    unnamed x3 -> x0, other arithmetic: 7.02 us -> none
    ppermute x4 -> x0, starting transfers between devices: 6.04 us -> none  [from_partner(): return lax.ppermute(value, axis, pairs)]
    unnamed x12 -> x1, local copies, waits for them, and re-layouts: 3.91 us -> 1.77 us
  transfers between devices with their start and end apart: 4 -> 0, of which waited for: 0 -> 0; matrix products, arithmetic and copies ran while one was open for 27% -> 0% of each run, Pallas kernels for 0% -> 0%
where the time goes in v1:
time: 20.9 us; the launch traced here: 20.8 us
  Pallas kernels  18.3 us (88%)
  local copies, waits for them, and re-layouts  1.77 us (8%)
  between operations  0.66 us (3%)
    pallas_call x1, Pallas kernels, local(): pl.pallas_call(functools.partial(kernel, bits, slots, blk), out_shape=jax...  18.3 us
    unnamed x1, local copies, waits for them, and re-layouts  1.77 us

profile of v1, /device:TPU:0, one launch (start us, length us, event | category | flops | bytes accessed | tf_op | source)
XLA Modules:
  0.0 20.8 jit_solution(9993334913828868316)
XLA Ops:
  0.7 18.3 %layer.1 = bf16[384,512]{1,0:T(8,128)(2,1)} custom-call(bf16[384,512]{1,0:T(8,128)(2,1)} %feat_hbm.1, bf16[3,512,512]{2,1,0:T(8,128)(2,1)} %bitcast.2, bf16[512,512]{1,0:T(8,128)(2,1)} %wo_hbm.1, bf16[512,1024]{1,0:T(8,128)(2,1)} %wu_hbm.1, bf16[1024,512]{1,0:T(8,128)(2,1)} %wd_hbm.1, s32[3,8,128]{2,1,0:T(8,128)} %bitcast.3, s32[3,4]{1,0:T(4,128)} %partner.1, ...), custom_call_target="tpu_custom_call" | custom-call | flops 5000000000 | bytes 10485760 | tf_op jit(solution)/shard_map/layer/pallas_call | solution.py:246
  19.0 1.8 %copy.11 = bf16[384,512]{1,0:T(8,128)(2,1)} copy(bf16[384,512]{1,0:T(8,128)(2,1)} %layer.1) | data formatting | bytes 786432

commit v2 on v1

--- a/solution.py
+++ b/solution.py
@@ -32,9 +32,9 @@
 
 def kernel(
     bits, slots, blk,
-    feat_hbm, w3_hbm, wo_hbm, wu_hbm, wd_hbm, pat_hbm, partner, counts,
+    feat_hbm, w3_hbm, wo_hbm, wu_hbm, wd_hbm, pat_hbm, partner_hbm, counts,
     out_ref,
-    x, w3, wo, wu, wd, pat, wqt, wvt, near, far,
+    partner, x, w3, wo, wu, wd, pat, wqt, wvt, near, far,
     qpad, kown, vown, knear, vnear, kfar, vfar,
     ob, mb, lb, of, mf, lf, att,
     load_sem, near_send, near_recv, far_send, far_recv,
@@ -49,7 +49,8 @@
 
     loads = []
     for i, (src, dst) in enumerate(
-        [(w3_hbm, w3), (feat_hbm, x), (pat_hbm, pat), (wo_hbm, wo), (wu_hbm, wu), (wd_hbm, wd)]
+        [(w3_hbm, w3), (feat_hbm, x), (pat_hbm, pat), (wo_hbm, wo), (wu_hbm, wu), (wd_hbm, wd),
+         (partner_hbm, partner)]
     ):
         loads.append(pltpu.make_async_copy(src, dst, load_sem.at[i]))
         loads[-1].start()
@@ -110,9 +111,27 @@
     project(own, setter(kown, lambda i: i), setter(vown, lambda i: i))
     near_copy.wait_recv()
     project(near[...], setter(knear, lambda i: i), setter(vnear, lambda i: i))
-    loads[2].wait()
-
-    def keep(o, m, l, o_ref, m_ref, l_ref, at, p):
+    for i in (2, 6):
+        loads[i].wait()
+
+    def run(units):
+        waiting = None
+        scores = units[0][0]()
+        for i, (_, values, put) in enumerate(units):
+            following = units[i + 1][0]() if i + 1 < len(units) else None
+            m = functools.reduce(jnp.maximum, [jnp.max(a, 0, keepdims=True) for a in scores])
+            expo = [jnp.exp(a - m) for a in scores]
+            l = functools.reduce(jnp.add, [jnp.sum(a, 0, keepdims=True) for a in expo])
+            expo = [a.astype(BF16) for a in expo]
+            if waiting is not None:
+                waiting()
+            waiting = functools.partial(
+                lambda values, put, expo, m, l: put(values(expo), m, l), values, put, expo, m, l
+            )
+            scores = following
+        waiting()
+
+    def keep(o_ref, m_ref, l_ref, at, p, o, m, l):
         o_ref[at + (pl.ds(2 * p * HD, HD),)] = o[:HD, :blk]
         o_ref[at + (pl.ds((2 * p + 1) * HD, HD),)] = o[HD:, blk:]
         for half in range(2):
@@ -123,6 +142,7 @@
     bit_row = lax.broadcasted_iota(jnp.int32, (16, blk), 0)
     key_at = lax.broadcasted_iota(jnp.int32, (blk, blk), 0)
     query_at = lax.broadcasted_iota(jnp.int32, (blk, blk), 1)
+    units = []
     for s in range(slots):
         words = pat[s]
         picked = jnp.concatenate(
@@ -139,18 +159,21 @@
         v1 = vnear[linked]
         for p in range(PAIRS):
             cols = slice(2 * p * HD, 2 * (p + 1) * HD)
-            q = qpad[s, p]
-            s0 = dot_nn(kown[s, :, cols], q) + bias
-            s1 = dot_nn(k1[:, cols], q)
-            m = jnp.maximum(jnp.max(s0, 0, keepdims=True), jnp.max(s1, 0, keepdims=True))
-            e0 = jnp.exp(s0 - m)
-            e1 = jnp.exp(s1 - m)
-            l = jnp.sum(e0, 0, keepdims=True) + jnp.sum(e1, 0, keepdims=True)
-            o = dot_nn(
-                jnp.concatenate([vown[s, cols], v1[cols]], 1),
-                jnp.concatenate([e0.astype(BF16), e1.astype(BF16)], 0),
-            )
-            keep(o, m, l, ob, mb, lb, (s,), p)
+
+            def scores(s=s, p=p, cols=cols, bias=bias, k1=k1):
+                q = qpad[s, p]
+                return [dot_nn(kown[s, :, cols], q) + bias, dot_nn(k1[:, cols], q)]
+
+            def values(e, s=s, cols=cols, v1=v1):
+                return dot_nn(
+                    jnp.concatenate([vown[s, cols], v1[cols]], 1), jnp.concatenate(e, 0)
+                )
+
+            units.append((scores, values, functools.partial(keep, ob, mb, lb, (s,), p)))
+    run(units)
+
+    for i in (3, 4, 5):
+        loads[i].wait()
 
     ranks, order = [], []
     for l in range(1, LINKS):
@@ -182,17 +205,20 @@
         for l in range(LINKS - 1):
             kfar[l, j] = k[l * blk : (l + 1) * blk]
             vfar[l, j] = v[:, l * blk : (l + 1) * blk]
+        units = []
         for l in range(LINKS - 1):
             slot, block = order[l][j]
-            kj = kfar[l, block]
-            vj = vfar[l, block]
             for p in range(PAIRS):
                 cols = slice(2 * p * HD, 2 * (p + 1) * HD)
-                scores = dot_nn(kj[:, cols], qpad[slot, p])
-                m = jnp.max(scores, 0, keepdims=True)
-                e = jnp.exp(scores - m)
-                o = dot_nn(vj[cols], e.astype(BF16))
-                keep(o, m, jnp.sum(e, 0, keepdims=True), of, mf, lf, (l, j), p)
+
+                def scores(l=l, slot=slot, block=block, p=p, cols=cols):
+                    return [dot_nn(kfar[l, block, :, cols], qpad[slot, p])]
+
+                def values(e, l=l, block=block, cols=cols):
+                    return dot_nn(vfar[l, block, cols], e[0])
+
+                units.append((scores, values, functools.partial(keep, of, mf, lf, (l, j), p)))
+        run(units)
 
     for s in range(slots):
         ms = [mb[s]] + [mf[l, ranks[l][s]] for l in range(LINKS - 1)]
@@ -209,10 +235,8 @@
                 [o[h * HD : (h + 1) * HD] * a[h : h + 1] for o, a in zip(os, scale)],
             ))
         joined = jnp.concatenate(heads, 0)
-        att[pl.ds(s * blk, blk)] = joined.T.astype(BF16)
-
-    for i in (3, 4, 5):
-        loads[i].wait()
+        att[pl.ds(s * blk, blk)] = joined.astype(BF16).T
+
     resid = x[...].astype(F32) + dot_nn(att[...], wo[...])
     mean = jnp.mean(resid, 1, keepdims=True)
     var = jnp.mean(resid * resid, 1, keepdims=True) - mean * mean
@@ -240,15 +264,22 @@
     bits = [i * log_size // 4 for i in range(LINKS)]
     far = LINKS - 1
     any_spec = pl.BlockSpec(memory_space=pl.ANY)
-    smem = pl.BlockSpec(memory_space=pltpu.SMEM)
     vm = pltpu.VMEM
     sem = pltpu.SemaphoreType.DMA
+    operands = [
+        pltpu.with_memory_space_constraint(a, pltpu.HBM)
+        for a in (
+            features, jnp.transpose(w_qkv, (1, 0, 2)), w_out, w_up, w_down,
+            jnp.transpose(pattern, (0, 2, 1)), partner,
+        )
+    ]
     return pl.pallas_call(
         functools.partial(kernel, bits, slots, blk),
-        out_shape=jax.ShapeDtypeStruct((rows, width), BF16),
-        in_specs=[any_spec] * 6 + [smem] * 2,
+        out_shape=pltpu.VMEM((rows, width), BF16),
+        in_specs=[any_spec] * 7 + [pl.BlockSpec(memory_space=pltpu.SMEM)],
         out_specs=pl.BlockSpec(memory_space=pltpu.VMEM),
         scratch_shapes=[
+            pltpu.SMEM(partner.shape, jnp.int32),
             vm((rows, width), BF16),
             vm((3, width, width), BF16),
             vm((width, width), BF16),
@@ -273,23 +304,20 @@
             vm((far, slots, H, blk), F32),
             vm((far, slots, H, blk), F32),
             vm((rows, width), BF16),
-            sem((6,)),
+            sem((7,)),
             sem,
             sem,
             sem((slots, far)),
             sem((slots, far)),
         ],
         compiler_params=pltpu.CompilerParams(
-            collective_id=0, has_side_effects=True, vmem_limit_bytes=60 * 2**20
+            collective_id=0, has_side_effects=True, vmem_limit_bytes=48 * 2**20
         ),
         cost_estimate=pl.CostEstimate(
             flops=5 * 10**9, bytes_accessed=10 * 2**20, transcendentals=2 * 10**6
         ),
         name="layer",
-    )(
-        features, jnp.transpose(w_qkv, (1, 0, 2)), w_out, w_up, w_down,
-        jnp.transpose(pattern, (0, 2, 1)), partner, counts,
-    )
+    )(*operands, counts)
 
 
 def solution(mesh):

time: 20.9 us -> 18.3 us (0.88)
  Pallas kernels: 18.3 us -> 16.7 us
  local copies, waits for them, and re-layouts: 1.77 us -> 0.75 us
    pallas_call x1, Pallas kernels: 18.3 us -> 16.7 us  [local(): pl.pallas_call(functools.partial(kernel, bits, slots, blk), out_shape=plt...]
    unnamed x1, local copies, waits for them, and re-layouts: 1.77 us -> 0.75 us
where the time goes in v2:
time: 18.3 us; the launch traced here: 18.1 us
  Pallas kernels  16.7 us (91%)
  local copies, waits for them, and re-layouts  0.75 us (4%)
  between operations  0.66 us (4%)
    pallas_call x1, Pallas kernels, local(): pl.pallas_call(functools.partial(kernel, bits, slots, blk), out_shape=plt...  16.7 us
    unnamed x1, local copies, waits for them, and re-layouts  0.75 us

profile of v2, /device:TPU:0, one launch (start us, length us, event | category | flops | bytes accessed | tf_op | source)
XLA Modules:
  0.0 18.1 jit_solution(4516665733356171601)
XLA Ops:
  0.7 16.7 %layer.1 = bf16[384,512]{1,0:T(8,128)(2,1)S(1)} custom-call(bf16[384,512]{1,0:T(8,128)(2,1)} %feat_hbm.1, bf16[3,512,512]{2,1,0:T(8,128)(2,1)} %bitcast.2, bf16[512,512]{1,0:T(8,128)(2,1)} %wo_hbm.1, bf16[512,1024]{1,0:T(8,128)(2,1)} %wu_hbm.1, bf16[1024,512]{1,0:T(8,128)(2,1)} %wd_hbm.1, s32[3,8,128]{2,1,0:T(8,128)} %bitcast.3, s32[3,4]{1,0:T(4,128)} %partner_hbm.1, ...), custom_call_target="tpu_custom_call" | custom-call | flops 5000000000 | bytes 10485760 | tf_op jit(solution)/shard_map/layer/pallas_call | solution.py:276
  17.4 0.7 %copy.10 = bf16[384,512]{1,0:T(8,128)(2,1)} copy(bf16[384,512]{1,0:T(8,128)(2,1)S(1)} %layer.1) | data formatting | bytes 786432

commit v3 on v2

--- a/solution.py
+++ b/solution.py
@@ -36,7 +36,7 @@
     out_ref,
     partner, x, w3, wo, wu, wd, pat, wqt, wvt, near, far,
     qpad, kown, vown, knear, vnear, kfar, vfar,
-    ob, mb, lb, of, mf, lf, att,
+    ob, mb, lb, of, mf, lf, nf, nb,
     load_sem, near_send, near_recv, far_send, far_recv,
 ):
     node = lax.axis_index("nodes")
@@ -76,7 +76,8 @@
                 send_sem=far_send.at[j, l], recv_sem=far_recv.at[j, l],
                 device_id=target(bits[l + 1]), device_id_type=pl.DeviceIdType.MESH,
             ))
-            row[-1].start()
+            if j < 2:
+                row[-1].start()
         far_copies.append(row)
         if j == 0:
             near_copy.start()
@@ -175,6 +176,11 @@
     for i in (3, 4, 5):
         loads[i].wait()
 
+    for j in range(2, slots):
+        for l in range(LINKS - 1):
+            far_copies[j - 2][l].wait_send()
+            far_copies[j][l].start()
+
     ranks, order = [], []
     for l in range(1, LINKS):
         named = [partner[s, l] for s in range(slots)]
@@ -235,21 +241,23 @@
                 [o[h * HD : (h + 1) * HD] * a[h : h + 1] for o, a in zip(os, scale)],
             ))
         joined = jnp.concatenate(heads, 0)
-        att[pl.ds(s * blk, blk)] = joined.astype(BF16).T
-
-    resid = x[...].astype(F32) + dot_nn(att[...], wo[...])
-    mean = jnp.mean(resid, 1, keepdims=True)
-    var = jnp.mean(resid * resid, 1, keepdims=True) - mean * mean
-    normed = (resid - mean) * lax.rsqrt(var + epsilon)
-    hidden = jnp.maximum(dot_nn(normed.astype(BF16), wu[...]), 0.0).astype(BF16)
-    mixed = normed + dot_nn(hidden, wd[...])
+        here = pl.ds(s * blk, blk)
+        resid = x[here].astype(F32) + dot_nn(joined.astype(BF16).T, wo[...])
+        mean = jnp.mean(resid, 1, keepdims=True)
+        var = jnp.mean(resid * resid, 1, keepdims=True) - mean * mean
+        normed = (resid - mean) * lax.rsqrt(var + epsilon)
+        nf[here] = normed
+        nb[here] = normed.astype(BF16)
+
+    hidden = jnp.maximum(dot_nn(nb[...], wu[...]), 0.0).astype(BF16)
+    mixed = nf[...] + dot_nn(hidden, wd[...])
     live = counts[0]
     for s in range(slots):
         part = mixed[s * blk : (s + 1) * blk]
         out_ref[pl.ds(s * blk, blk)] = jnp.where(s < live, part, 0.0).astype(BF16)
 
     near_copy.wait_send()
-    for row in far_copies:
+    for row in far_copies[max(slots - 2, 0):]:
         for copy in row:
             copy.wait_send()
 
@@ -303,6 +311,7 @@
             vm((far, slots, width, blk), F32),
             vm((far, slots, H, blk), F32),
             vm((far, slots, H, blk), F32),
+            vm((rows, width), F32),
             vm((rows, width), BF16),
             sem((7,)),
             sem,

time: 18.3 us -> 18.3 us (level)
  no operation moved by 1% of the time
where the time goes in v3:
time: 18.3 us; the launch traced here: 18.1 us
  Pallas kernels  16.7 us (91%)
  local copies, waits for them, and re-layouts  0.75 us (4%)
  between operations  0.66 us (4%)
    pallas_call x1, Pallas kernels, local(): pl.pallas_call(functools.partial(kernel, bits, slots, blk), out_shape=plt...  16.7 us
    unnamed x1, local copies, waits for them, and re-layouts  0.75 us

profile of v3, /device:TPU:0, one launch (start us, length us, event | category | flops | bytes accessed | tf_op | source)
XLA Modules:
  0.0 18.1 jit_solution(18057197884352575507)
XLA Ops:
  0.7 16.7 %layer.1 = bf16[384,512]{1,0:T(8,128)(2,1)S(1)} custom-call(bf16[384,512]{1,0:T(8,128)(2,1)} %feat_hbm.1, bf16[3,512,512]{2,1,0:T(8,128)(2,1)} %bitcast.2, bf16[512,512]{1,0:T(8,128)(2,1)} %wo_hbm.1, bf16[512,1024]{1,0:T(8,128)(2,1)} %wu_hbm.1, bf16[1024,512]{1,0:T(8,128)(2,1)} %wd_hbm.1, s32[3,8,128]{2,1,0:T(8,128)} %bitcast.3, s32[3,4]{1,0:T(4,128)} %partner_hbm.1, ...), custom_call_target="tpu_custom_call" | custom-call | flops 5000000000 | bytes 10485760 | tf_op jit(solution)/shard_map/layer/pallas_call | solution.py:284
  17.4 0.7 %copy.10 = bf16[384,512]{1,0:T(8,128)(2,1)} copy(bf16[384,512]{1,0:T(8,128)(2,1)S(1)} %layer.1) | data formatting | bytes 786432

commit v4 on v3

--- a/solution.py
+++ b/solution.py
@@ -96,22 +96,15 @@
             qpad[s, p] = jnp.concatenate(
                 [jnp.concatenate([a, zero], 1), jnp.concatenate([zero, b], 1)], 0
             )
-
-    def project(rows, put_k, put_v):
-        k = dot_nn(rows, w3[1]).astype(BF16)
-        v = dot_nt(wvt[...], rows).astype(BF16)
-        for i in range(slots):
-            put_k(i, k[i * blk : (i + 1) * blk])
-            put_v(i, v[:, i * blk : (i + 1) * blk])
-
-    def setter(ref, where):
-        def put(i, value):
-            ref[where(i)] = value
-        return put
-
-    project(own, setter(kown, lambda i: i), setter(vown, lambda i: i))
     near_copy.wait_recv()
-    project(near[...], setter(knear, lambda i: i), setter(vnear, lambda i: i))
+    both = jnp.concatenate([own, near[...]], 0)
+    k = dot_nn(both, w3[1]).astype(BF16)
+    v = dot_nt(wvt[...], both).astype(BF16)
+    for i in range(slots):
+        kown[i] = k[i * blk : (i + 1) * blk]
+        vown[i] = v[:, i * blk : (i + 1) * blk]
+        knear[i] = k[(slots + i) * blk : (slots + i + 1) * blk]
+        vnear[i] = v[:, (slots + i) * blk : (slots + i + 1) * blk]
     for i in (2, 6):
         loads[i].wait()
 
@@ -162,8 +155,8 @@
             cols = slice(2 * p * HD, 2 * (p + 1) * HD)
 
             def scores(s=s, p=p, cols=cols, bias=bias, k1=k1):
-                q = qpad[s, p]
-                return [dot_nn(kown[s, :, cols], q) + bias, dot_nn(k1[:, cols], q)]
+                both = dot_nn(jnp.concatenate([kown[s, :, cols], k1[:, cols]], 0), qpad[s, p])
+                return [both[:blk] + bias, both[blk:]]
 
             def values(e, s=s, cols=cols, v1=v1):
                 return dot_nn(

time: 18.3 us -> 18.3 us (level)
  no operation moved by 1% of the time
where the time goes in v4:
time: 18.3 us; the launch traced here: 18.1 us
  Pallas kernels  16.7 us (91%)
  local copies, waits for them, and re-layouts  0.75 us (4%)
  between operations  0.66 us (4%)
    pallas_call x1, Pallas kernels, local(): pl.pallas_call(functools.partial(kernel, bits, slots, blk), out_shape=plt...  16.7 us
    unnamed x1, local copies, waits for them, and re-layouts  0.75 us

profile of v4, /device:TPU:0, one launch (start us, length us, event | category | flops | bytes accessed | tf_op | source)
XLA Modules:
  0.0 18.1 jit_solution(11444537156019586370)
XLA Ops:
  0.7 16.7 %layer.1 = bf16[384,512]{1,0:T(8,128)(2,1)S(1)} custom-call(bf16[384,512]{1,0:T(8,128)(2,1)} %feat_hbm.1, bf16[3,512,512]{2,1,0:T(8,128)(2,1)} %bitcast.2, bf16[512,512]{1,0:T(8,128)(2,1)} %wo_hbm.1, bf16[512,1024]{1,0:T(8,128)(2,1)} %wu_hbm.1, bf16[1024,512]{1,0:T(8,128)(2,1)} %wd_hbm.1, s32[3,8,128]{2,1,0:T(8,128)} %bitcast.3, s32[3,4]{1,0:T(4,128)} %partner_hbm.1, ...), custom_call_target="tpu_custom_call" | custom-call | flops 5000000000 | bytes 10485760 | tf_op jit(solution)/shard_map/layer/pallas_call | solution.py:277
  17.4 0.7 %copy.10 = bf16[384,512]{1,0:T(8,128)(2,1)} copy(bf16[384,512]{1,0:T(8,128)(2,1)S(1)} %layer.1) | data formatting | bytes 786432

commit v5 on v4

--- a/solution.py
+++ b/solution.py
@@ -47,6 +47,11 @@
             return (node, flip(core, 1))
         return (flip(node, 2 ** (bit - 1)), core)
 
+    barrier = pltpu.get_barrier_semaphore()
+    for bit in bits:
+        pl.semaphore_signal(
+            barrier, inc=1, device_id=target(bit), device_id_type=pl.DeviceIdType.MESH
+        )
     loads = []
     for i, (src, dst) in enumerate(
         [(w3_hbm, w3), (feat_hbm, x), (pat_hbm, pat), (wo_hbm, wo), (wu_hbm, wu), (wd_hbm, wd),
@@ -55,11 +60,6 @@
         loads.append(pltpu.make_async_copy(src, dst, load_sem.at[i]))
         loads[-1].start()
 
-    barrier = pltpu.get_barrier_semaphore()
-    for bit in bits:
-        pl.semaphore_signal(
-            barrier, inc=1, device_id=target(bit), device_id_type=pl.DeviceIdType.MESH
-        )
     pl.semaphore_wait(barrier, LINKS)
 
     far_copies = []
@@ -67,19 +67,21 @@
         src_ref=feat_hbm, dst_ref=near, send_sem=near_send, recv_sem=near_recv,
         device_id=target(bits[0]), device_id_type=pl.DeviceIdType.MESH,
     )
-    for j in range(slots):
+    half = blk // 2
+    pieces = [(j, 0, blk) for j in range(slots - 1)]
+    pieces += [(slots - 1, 0, half), (slots - 1, half, half)]
+    for n, (j, start, size) in enumerate(pieces):
         row = []
         for l in range(LINKS - 1):
             row.append(pltpu.make_async_remote_copy(
-                src_ref=feat_hbm.at[pl.ds(j * blk, blk)],
-                dst_ref=far.at[j, pl.ds(l * blk, blk)],
-                send_sem=far_send.at[j, l], recv_sem=far_recv.at[j, l],
+                src_ref=feat_hbm.at[pl.ds(j * blk + start, size)],
+                dst_ref=far.at[j, pl.ds((LINKS - 1) * start + l * size, size)],
+                send_sem=far_send.at[n, l], recv_sem=far_recv.at[n, l],
                 device_id=target(bits[l + 1]), device_id_type=pl.DeviceIdType.MESH,
             ))
-            if j < 2:
-                row[-1].start()
+            row[-1].start()
         far_copies.append(row)
-        if j == 0:
+        if n == 0:
             near_copy.start()
 
     loads[0].wait()
@@ -96,15 +98,16 @@
             qpad[s, p] = jnp.concatenate(
                 [jnp.concatenate([a, zero], 1), jnp.concatenate([zero, b], 1)], 0
             )
+    def project(rows, k_ref, v_ref):
+        k = dot_nn(rows, w3[1]).astype(BF16)
+        v = dot_nt(wvt[...], rows).astype(BF16)
+        for i in range(slots):
+            k_ref[i] = k[i * blk : (i + 1) * blk]
+            v_ref[i] = v[:, i * blk : (i + 1) * blk]
+
+    project(own, kown, vown)
     near_copy.wait_recv()
-    both = jnp.concatenate([own, near[...]], 0)
-    k = dot_nn(both, w3[1]).astype(BF16)
-    v = dot_nt(wvt[...], both).astype(BF16)
-    for i in range(slots):
-        kown[i] = k[i * blk : (i + 1) * blk]
-        vown[i] = v[:, i * blk : (i + 1) * blk]
-        knear[i] = k[(slots + i) * blk : (slots + i + 1) * blk]
-        vnear[i] = v[:, (slots + i) * blk : (slots + i + 1) * blk]
+    project(near[...], knear, vnear)
     for i in (2, 6):
         loads[i].wait()
 
@@ -169,11 +172,6 @@
     for i in (3, 4, 5):
         loads[i].wait()
 
-    for j in range(2, slots):
-        for l in range(LINKS - 1):
-            far_copies[j - 2][l].wait_send()
-            far_copies[j][l].start()
-
     ranks, order = [], []
     for l in range(1, LINKS):
         named = [partner[s, l] for s in range(slots)]
@@ -195,28 +193,51 @@
         ranks.append(rank)
         order.append(at)
 
-    for j in range(slots):
+    def merge(o_ref, m_ref, l_ref, at, p, o, m, l):
+        for side in range(2):
+            h = 2 * p + side
+            cols = slice(side * blk, (side + 1) * blk)
+            rows = at + (pl.ds(h * HD, HD),)
+            row = at + (pl.ds(h, 1),)
+            before = m_ref[row]
+            top = jnp.maximum(before, m[:, cols])
+            old, new = jnp.exp(before - top), jnp.exp(m[:, cols] - top)
+            o_ref[rows] = o_ref[rows] * old + o[side * HD : (side + 1) * HD, cols] * new
+            l_ref[row] = l_ref[row] * old + l[:, cols] * new
+            m_ref[row] = top
+
+    for n, (j, start, size) in enumerate(pieces):
         for l in range(LINKS - 1):
-            far_copies[j][l].wait_recv()
-        rows = far[j]
+            far_copies[n][l].wait_recv()
+        rows = far[j, pl.ds((LINKS - 1) * start, (LINKS - 1) * size)]
         k = dot_nn(rows, w3[1]).astype(BF16)
         v = dot_nt(wvt[...], rows).astype(BF16)
         for l in range(LINKS - 1):
-            kfar[l, j] = k[l * blk : (l + 1) * blk]
-            vfar[l, j] = v[:, l * blk : (l + 1) * blk]
+            vl = v[:, l * size : (l + 1) * size]
+            kfar[l, j, pl.ds(start, size)] = k[l * size : (l + 1) * size]
+            if size < blk and start == 0:
+                vl = jnp.concatenate([vl, jnp.zeros((D, blk - size), BF16)], 1)
+                vfar[l, j] = vl
+            else:
+                vfar[l, j, :, pl.ds(start, size)] = vl
         units = []
         for l in range(LINKS - 1):
             slot, block = order[l][j]
             for p in range(PAIRS):
                 cols = slice(2 * p * HD, 2 * (p + 1) * HD)
 
-                def scores(l=l, slot=slot, block=block, p=p, cols=cols):
-                    return [dot_nn(kfar[l, block, :, cols], qpad[slot, p])]
-
-                def values(e, l=l, block=block, cols=cols):
-                    return dot_nn(vfar[l, block, cols], e[0])
-
-                units.append((scores, values, functools.partial(keep, of, mf, lf, (l, j), p)))
+                def scores(l=l, slot=slot, block=block, p=p, cols=cols, rows=pl.ds(start, size)):
+                    return [dot_nn(kfar[l, block, rows, cols], qpad[slot, p])]
+
+                def values(e, l=l, block=block, cols=cols, start=start, size=size):
+                    parts = [e[0]]
+                    if size < blk:
+                        rest = jnp.zeros((blk - size, 2 * blk), BF16)
+                        parts = [rest] + parts if start else parts + [rest]
+                    return dot_nn(vfar[l, block, cols], jnp.concatenate(parts, 0))
+
+                put = merge if start else keep
+                units.append((scores, values, functools.partial(put, of, mf, lf, (l, j), p)))
         run(units)
 
     for s in range(slots):
@@ -250,7 +271,7 @@
         out_ref[pl.ds(s * blk, blk)] = jnp.where(s < live, part, 0.0).astype(BF16)
 
     near_copy.wait_send()
-    for row in far_copies[max(slots - 2, 0):]:
+    for row in far_copies:
         for copy in row:
             copy.wait_send()
 
@@ -309,8 +330,8 @@
             sem((7,)),
             sem,
             sem,
-            sem((slots, far)),
-            sem((slots, far)),
+            sem((slots + 1, far)),
+            sem((slots + 1, far)),
         ],
         compiler_params=pltpu.CompilerParams(
             collective_id=0, has_side_effects=True, vmem_limit_bytes=48 * 2**20

time: 18.3 us -> 19.5 us (1.066)
  Pallas kernels: 16.7 us -> 17.9 us
    pallas_call x1, Pallas kernels: 16.7 us -> 17.9 us  [local(): pl.pallas_call(functools.partial(kernel, bits, slots, blk), out_shape=plt...]
where the time goes in v5:
time: 19.5 us; the launch traced here: 19.3 us
  Pallas kernels  17.9 us (92%)
  local copies, waits for them, and re-layouts  0.75 us (4%)
  between operations  0.66 us (3%)
    pallas_call x1, Pallas kernels, local(): pl.pallas_call(functools.partial(kernel, bits, slots, blk), out_shape=plt...  17.9 us
    unnamed x1, local copies, waits for them, and re-layouts  0.75 us

profile of v5, /device:TPU:0, one launch (start us, length us, event | category | flops | bytes accessed | tf_op | source)
XLA Modules:
  0.0 19.3 jit_solution(12797303724530300333)
XLA Ops:
  0.7 17.9 %layer.1 = bf16[384,512]{1,0:T(8,128)(2,1)S(1)} custom-call(bf16[384,512]{1,0:T(8,128)(2,1)} %feat_hbm.1, bf16[3,512,512]{2,1,0:T(8,128)(2,1)} %bitcast.2, bf16[512,512]{1,0:T(8,128)(2,1)} %wo_hbm.1, bf16[512,1024]{1,0:T(8,128)(2,1)} %wu_hbm.1, bf16[1024,512]{1,0:T(8,128)(2,1)} %wd_hbm.1, s32[3,8,128]{2,1,0:T(8,128)} %bitcast.3, s32[3,4]{1,0:T(4,128)} %partner_hbm.1, ...), custom_call_target="tpu_custom_call" | custom-call | flops 5000000000 | bytes 10485760 | tf_op jit(solution)/shard_map/layer/pallas_call | solution.py:298
  18.6 0.7 %copy.10 = bf16[384,512]{1,0:T(8,128)(2,1)} copy(bf16[384,512]{1,0:T(8,128)(2,1)S(1)} %layer.1) | data formatting | bytes 786432

commit v6 on v2

--- a/solution.py
+++ b/solution.py
@@ -36,7 +36,7 @@
     out_ref,
     partner, x, w3, wo, wu, wd, pat, wqt, wvt, near, far,
     qpad, kown, vown, knear, vnear, kfar, vfar,
-    ob, mb, lb, of, mf, lf, att,
+    ob, mb, lb, of, mf, lf, nb,
     load_sem, near_send, near_recv, far_send, far_recv,
 ):
     node = lax.axis_index("nodes")
@@ -47,6 +47,11 @@
             return (node, flip(core, 1))
         return (flip(node, 2 ** (bit - 1)), core)
 
+    barrier = pltpu.get_barrier_semaphore()
+    for bit in bits:
+        pl.semaphore_signal(
+            barrier, inc=1, device_id=target(bit), device_id_type=pl.DeviceIdType.MESH
+        )
     loads = []
     for i, (src, dst) in enumerate(
         [(w3_hbm, w3), (feat_hbm, x), (pat_hbm, pat), (wo_hbm, wo), (wu_hbm, wu), (wd_hbm, wd),
@@ -55,29 +60,23 @@
         loads.append(pltpu.make_async_copy(src, dst, load_sem.at[i]))
         loads[-1].start()
 
-    barrier = pltpu.get_barrier_semaphore()
-    for bit in bits:
-        pl.semaphore_signal(
-            barrier, inc=1, device_id=target(bit), device_id_type=pl.DeviceIdType.MESH
+    pl.semaphore_wait(barrier, LINKS)
+
+    def far_copy(j, l):
+        return pltpu.make_async_remote_copy(
+            src_ref=feat_hbm.at[pl.ds(pl.multiple_of(j * blk, blk), blk)],
+            dst_ref=far.at[j, pl.ds(l * blk, blk)],
+            send_sem=far_send.at[j, l], recv_sem=far_recv.at[j, l],
+            device_id=target(bits[l + 1]), device_id_type=pl.DeviceIdType.MESH,
         )
-    pl.semaphore_wait(barrier, LINKS)
-
-    far_copies = []
+
     near_copy = pltpu.make_async_remote_copy(
         src_ref=feat_hbm, dst_ref=near, send_sem=near_send, recv_sem=near_recv,
         device_id=target(bits[0]), device_id_type=pl.DeviceIdType.MESH,
     )
     for j in range(slots):
-        row = []
-        for l in range(LINKS - 1):
-            row.append(pltpu.make_async_remote_copy(
-                src_ref=feat_hbm.at[pl.ds(j * blk, blk)],
-                dst_ref=far.at[j, pl.ds(l * blk, blk)],
-                send_sem=far_send.at[j, l], recv_sem=far_recv.at[j, l],
-                device_id=target(bits[l + 1]), device_id_type=pl.DeviceIdType.MESH,
-            ))
-            row[-1].start()
-        far_copies.append(row)
+        for l in range(LINKS - 1):
+            far_copy(j, l).start()
         if j == 0:
             near_copy.start()
 
@@ -142,8 +141,7 @@
     bit_row = lax.broadcasted_iota(jnp.int32, (16, blk), 0)
     key_at = lax.broadcasted_iota(jnp.int32, (blk, blk), 0)
     query_at = lax.broadcasted_iota(jnp.int32, (blk, blk), 1)
-    units = []
-    for s in range(slots):
+    def attend_base(s, carry):
         words = pat[s]
         picked = jnp.concatenate(
             [
@@ -155,22 +153,26 @@
         bias = jnp.where((picked == 1) | (key_at == query_at), 0.0, -1e30).astype(F32)
         bias = jnp.concatenate([bias, bias], 1)
         linked = partner[s, 0]
-        k1 = knear[linked]
-        v1 = vnear[linked]
+        units = []
         for p in range(PAIRS):
             cols = slice(2 * p * HD, 2 * (p + 1) * HD)
 
-            def scores(s=s, p=p, cols=cols, bias=bias, k1=k1):
-                q = qpad[s, p]
-                return [dot_nn(kown[s, :, cols], q) + bias, dot_nn(k1[:, cols], q)]
-
-            def values(e, s=s, cols=cols, v1=v1):
+            def scores(p=p, cols=cols):
+                keys = jnp.concatenate([kown[s, :, cols], knear[linked, :, cols]], 0)
+                both = dot_nn(keys, qpad[s, p])
+                return [both[:blk] + bias, both[blk:]]
+
+            def values(e, cols=cols):
                 return dot_nn(
-                    jnp.concatenate([vown[s, cols], v1[cols]], 1), jnp.concatenate(e, 0)
+                    jnp.concatenate([vown[s, cols], vnear[linked, cols]], 1),
+                    jnp.concatenate(e, 0),
                 )
 
             units.append((scores, values, functools.partial(keep, ob, mb, lb, (s,), p)))
-    run(units)
+        run(units)
+        return carry
+
+    lax.fori_loop(0, slots, attend_base, 0)
 
     for i in (3, 4, 5):
         loads[i].wait()
@@ -196,9 +198,15 @@
         ranks.append(rank)
         order.append(at)
 
-    for j in range(slots):
-        for l in range(LINKS - 1):
-            far_copies[j][l].wait_recv()
+    def pick(j, choices):
+        result = choices[-1]
+        for i in range(len(choices) - 1):
+            result = jnp.where(j == i, choices[i], result)
+        return result
+
+    def attend_far(j, carry):
+        for l in range(LINKS - 1):
+            far_copy(j, l).wait_recv()
         rows = far[j]
         k = dot_nn(rows, w3[1]).astype(BF16)
         v = dot_nt(wvt[...], rows).astype(BF16)
@@ -207,7 +215,8 @@
             vfar[l, j] = v[:, l * blk : (l + 1) * blk]
         units = []
         for l in range(LINKS - 1):
-            slot, block = order[l][j]
+            slot = pick(j, [a for a, _ in order[l]])
+            block = pick(j, [a for _, a in order[l]])
             for p in range(PAIRS):
                 cols = slice(2 * p * HD, 2 * (p + 1) * HD)
 
@@ -219,25 +228,32 @@
 
                 units.append((scores, values, functools.partial(keep, of, mf, lf, (l, j), p)))
         run(units)
-
-    for s in range(slots):
-        ms = [mb[s]] + [mf[l, ranks[l][s]] for l in range(LINKS - 1)]
-        ls = [lb[s]] + [lf[l, ranks[l][s]] for l in range(LINKS - 1)]
-        os = [ob[s]] + [of[l, ranks[l][s]] for l in range(LINKS - 1)]
+        return carry
+
+    lax.fori_loop(0, slots, attend_far, 0)
+
+    def join(s, carry):
+        at = [pick(s, ranks[l]) for l in range(LINKS - 1)]
+        ms = [mb[s]] + [mf[l, at[l]] for l in range(LINKS - 1)]
+        ls = [lb[s]] + [lf[l, at[l]] for l in range(LINKS - 1)]
         top = functools.reduce(jnp.maximum, ms)
         scale = [jnp.exp(m - top) for m in ms]
         total = functools.reduce(jnp.add, [a * b for a, b in zip(scale, ls)])
         scale = [a / total for a in scale]
         heads = []
         for h in range(H):
+            rows = pl.ds(h * HD, HD)
+            os = [ob[s, rows]] + [of[l, at[l], rows] for l in range(LINKS - 1)]
             heads.append(functools.reduce(
-                jnp.add,
-                [o[h * HD : (h + 1) * HD] * a[h : h + 1] for o, a in zip(os, scale)],
+                jnp.add, [o * a[h : h + 1] for o, a in zip(os, scale)]
             ))
-        joined = jnp.concatenate(heads, 0)
-        att[pl.ds(s * blk, blk)] = joined.astype(BF16).T
-
-    resid = x[...].astype(F32) + dot_nn(att[...], wo[...])
+        joined = jnp.concatenate(heads, 0).astype(BF16).T
+        nb[pl.ds(pl.multiple_of(s * blk, blk), blk)] = joined
+        return carry
+
+    lax.fori_loop(0, slots, join, 0)
+
+    resid = x[...].astype(F32) + dot_nn(nb[...], wo[...])
     mean = jnp.mean(resid, 1, keepdims=True)
     var = jnp.mean(resid * resid, 1, keepdims=True) - mean * mean
     normed = (resid - mean) * lax.rsqrt(var + epsilon)
@@ -249,9 +265,9 @@
         out_ref[pl.ds(s * blk, blk)] = jnp.where(s < live, part, 0.0).astype(BF16)
 
     near_copy.wait_send()
-    for row in far_copies:
-        for copy in row:
-            copy.wait_send()
+    for j in range(slots):
+        for l in range(LINKS - 1):
+            far_copy(j, l).wait_send()
 
 
 def local(features, w_qkv, w_out, w_up, w_down, pattern, partner, counts):

time: 18.3 us -> 18.5 us (1.011)
  Pallas kernels: 16.7 us -> 17 us
    pallas_call x1, Pallas kernels: 16.7 us -> 17 us  [local(): pl.pallas_call(functools.partial(kernel, bits, slots, blk), out_shape=plt...]
where the time goes in v6:
time: 18.5 us; the launch traced here: 18.4 us
  Pallas kernels  17 us (92%)
  local copies, waits for them, and re-layouts  0.75 us (4%)
  between operations  0.66 us (4%)
    pallas_call x1, Pallas kernels, local(): pl.pallas_call(functools.partial(kernel, bits, slots, blk), out_shape=plt...  17 us
    unnamed x1, local copies, waits for them, and re-layouts  0.75 us

profile of v6, /device:TPU:0, one launch (start us, length us, event | category | flops | bytes accessed | tf_op | source)
XLA Modules:
  0.0 18.4 jit_solution(4917419775838549686)
XLA Ops:
  0.7 17.0 %layer.1 = bf16[384,512]{1,0:T(8,128)(2,1)S(1)} custom-call(bf16[384,512]{1,0:T(8,128)(2,1)} %feat_hbm.1, bf16[3,512,512]{2,1,0:T(8,128)(2,1)} %bitcast.2, bf16[512,512]{1,0:T(8,128)(2,1)} %wo_hbm.1, bf16[512,1024]{1,0:T(8,128)(2,1)} %wu_hbm.1, bf16[1024,512]{1,0:T(8,128)(2,1)} %wd_hbm.1, s32[3,8,128]{2,1,0:T(8,128)} %bitcast.3, s32[3,4]{1,0:T(4,128)} %partner_hbm.1, ...), custom_call_target="tpu_custom_call" | custom-call | flops 5000000000 | bytes 10485760 | tf_op jit(solution)/shard_map/layer/pallas_call | solution.py:292
  17.6 0.7 %copy.10 = bf16[384,512]{1,0:T(8,128)(2,1)} copy(bf16[384,512]{1,0:T(8,128)(2,1)S(1)} %layer.1) | data formatting | bytes 786432

commit v7 on v3

--- a/solution.py
+++ b/solution.py
@@ -47,6 +47,11 @@
             return (node, flip(core, 1))
         return (flip(node, 2 ** (bit - 1)), core)
 
+    barrier = pltpu.get_barrier_semaphore()
+    for bit in bits:
+        pl.semaphore_signal(
+            barrier, inc=1, device_id=target(bit), device_id_type=pl.DeviceIdType.MESH
+        )
     loads = []
     for i, (src, dst) in enumerate(
         [(w3_hbm, w3), (feat_hbm, x), (pat_hbm, pat), (wo_hbm, wo), (wu_hbm, wu), (wd_hbm, wd),
@@ -55,11 +60,6 @@
         loads.append(pltpu.make_async_copy(src, dst, load_sem.at[i]))
         loads[-1].start()
 
-    barrier = pltpu.get_barrier_semaphore()
-    for bit in bits:
-        pl.semaphore_signal(
-            barrier, inc=1, device_id=target(bit), device_id_type=pl.DeviceIdType.MESH
-        )
     pl.semaphore_wait(barrier, LINKS)
 
     far_copies = []
@@ -67,19 +67,19 @@
         src_ref=feat_hbm, dst_ref=near, send_sem=near_send, recv_sem=near_recv,
         device_id=target(bits[0]), device_id_type=pl.DeviceIdType.MESH,
     )
-    for j in range(slots):
+    pieces = [(0, slots - 1), (slots - 1, 1)]
+    for n, (first, count) in enumerate(pieces):
         row = []
         for l in range(LINKS - 1):
             row.append(pltpu.make_async_remote_copy(
-                src_ref=feat_hbm.at[pl.ds(j * blk, blk)],
-                dst_ref=far.at[j, pl.ds(l * blk, blk)],
-                send_sem=far_send.at[j, l], recv_sem=far_recv.at[j, l],
+                src_ref=feat_hbm.at[pl.ds(first * blk, count * blk)],
+                dst_ref=far.at[pl.ds(((LINKS - 1) * first + l * count) * blk, count * blk)],
+                send_sem=far_send.at[n, l], recv_sem=far_recv.at[n, l],
                 device_id=target(bits[l + 1]), device_id_type=pl.DeviceIdType.MESH,
             ))
-            if j < 2:
-                row[-1].start()
+            row[-1].start()
         far_copies.append(row)
-        if j == 0:
+        if n == 0:
             near_copy.start()
 
     loads[0].wait()
@@ -176,11 +176,6 @@
     for i in (3, 4, 5):
         loads[i].wait()
 
-    for j in range(2, slots):
-        for l in range(LINKS - 1):
-            far_copies[j - 2][l].wait_send()
-            far_copies[j][l].start()
-
     ranks, order = [], []
     for l in range(1, LINKS):
         named = [partner[s, l] for s in range(slots)]
@@ -202,28 +197,31 @@
         ranks.append(rank)
         order.append(at)
 
-    for j in range(slots):
+    for n, (first, count) in enumerate(pieces):
         for l in range(LINKS - 1):
-            far_copies[j][l].wait_recv()
-        rows = far[j]
+            far_copies[n][l].wait_recv()
+        rows = far[pl.ds((LINKS - 1) * first * blk, (LINKS - 1) * count * blk)]
         k = dot_nn(rows, w3[1]).astype(BF16)
         v = dot_nt(wvt[...], rows).astype(BF16)
         for l in range(LINKS - 1):
-            kfar[l, j] = k[l * blk : (l + 1) * blk]
-            vfar[l, j] = v[:, l * blk : (l + 1) * blk]
+            for i in range(count):
+                at = (l * count + i) * blk
+                kfar[l, first + i] = k[at : at + blk]
+                vfar[l, first + i] = v[:, at : at + blk]
         units = []
-        for l in range(LINKS - 1):
-            slot, block = order[l][j]
-            for p in range(PAIRS):
-                cols = slice(2 * p * HD, 2 * (p + 1) * HD)
-
-                def scores(l=l, slot=slot, block=block, p=p, cols=cols):
-                    return [dot_nn(kfar[l, block, :, cols], qpad[slot, p])]
-
-                def values(e, l=l, block=block, cols=cols):
-                    return dot_nn(vfar[l, block, cols], e[0])
-
-                units.append((scores, values, functools.partial(keep, of, mf, lf, (l, j), p)))
+        for j in range(first, first + count):
+            for l in range(LINKS - 1):
+                slot, block = order[l][j]
+                for p in range(PAIRS):
+                    cols = slice(2 * p * HD, 2 * (p + 1) * HD)
+
+                    def scores(l=l, slot=slot, block=block, p=p, cols=cols):
+                        return [dot_nn(kfar[l, block, :, cols], qpad[slot, p])]
+
+                    def values(e, l=l, block=block, cols=cols):
+                        return dot_nn(vfar[l, block, cols], e[0])
+
+                    units.append((scores, values, functools.partial(keep, of, mf, lf, (l, j), p)))
         run(units)
 
     for s in range(slots):
@@ -257,7 +255,7 @@
         out_ref[pl.ds(s * blk, blk)] = jnp.where(s < live, part, 0.0).astype(BF16)
 
     near_copy.wait_send()
-    for row in far_copies[max(slots - 2, 0):]:
+    for row in far_copies:
         for copy in row:
             copy.wait_send()
 
@@ -297,7 +295,7 @@
             vm((width, width), BF16),
             vm((width, width), BF16),
             vm((rows, width), BF16),
-            vm((slots, far * blk, width), BF16),
+            vm((slots * far * blk, width), BF16),
             vm((slots, PAIRS, 2 * HD, 2 * blk), BF16),
             vm((slots, blk, width), BF16),
             vm((slots, width, blk), BF16),
@@ -316,8 +314,8 @@
             sem((7,)),
             sem,
             sem,
-            sem((slots, far)),
-            sem((slots, far)),
+            sem((2, far)),
+            sem((2, far)),
         ],
         compiler_params=pltpu.CompilerParams(
             collective_id=0, has_side_effects=True, vmem_limit_bytes=48 * 2**20

time: 18.3 us -> 18.8 us (1.027)
  Pallas kernels: 16.7 us -> 17.3 us
    pallas_call x1, Pallas kernels: 16.7 us -> 17.3 us  [local(): pl.pallas_call(functools.partial(kernel, bits, slots, blk), out_shape=plt...]
where the time goes in v7:
time: 18.8 us; the launch traced here: 18.7 us
  Pallas kernels  17.3 us (92%)
  local copies, waits for them, and re-layouts  0.75 us (4%)
  between operations  0.66 us (4%)
    pallas_call x1, Pallas kernels, local(): pl.pallas_call(functools.partial(kernel, bits, slots, blk), out_shape=plt...  17.3 us
    unnamed x1, local copies, waits for them, and re-layouts  0.75 us

profile of v7, /device:TPU:0, one launch (start us, length us, event | category | flops | bytes accessed | tf_op | source)
XLA Modules:
  0.0 18.7 jit_solution(8404479339629319475)
XLA Ops:
  0.7 17.3 %layer.1 = bf16[384,512]{1,0:T(8,128)(2,1)S(1)} custom-call(bf16[384,512]{1,0:T(8,128)(2,1)} %feat_hbm.1, bf16[3,512,512]{2,1,0:T(8,128)(2,1)} %bitcast.2, bf16[512,512]{1,0:T(8,128)(2,1)} %wo_hbm.1, bf16[512,1024]{1,0:T(8,128)(2,1)} %wu_hbm.1, bf16[1024,512]{1,0:T(8,128)(2,1)} %wd_hbm.1, s32[3,8,128]{2,1,0:T(8,128)} %bitcast.3, s32[3,4]{1,0:T(4,128)} %partner_hbm.1, ...), custom_call_target="tpu_custom_call" | custom-call | flops 5000000000 | bytes 10485760 | tf_op jit(solution)/shard_map/layer/pallas_call | solution.py:282
  17.9 0.7 %copy.10 = bf16[384,512]{1,0:T(8,128)(2,1)} copy(bf16[384,512]{1,0:T(8,128)(2,1)S(1)} %layer.1) | data formatting | bytes 786432

commit v8 on v3

--- a/solution.py
+++ b/solution.py
@@ -116,21 +116,23 @@
         loads[i].wait()
 
     def run(units):
-        waiting = None
-        scores = units[0][0]()
+        ahead, behind = 2, 2
+        waiting = []
+        ready = [unit[0]() for unit in units[:ahead]]
         for i, (_, values, put) in enumerate(units):
-            following = units[i + 1][0]() if i + 1 < len(units) else None
+            if i + ahead < len(units):
+                ready.append(units[i + ahead][0]())
+            scores = ready.pop(0)
             m = functools.reduce(jnp.maximum, [jnp.max(a, 0, keepdims=True) for a in scores])
             expo = [jnp.exp(a - m) for a in scores]
             l = functools.reduce(jnp.add, [jnp.sum(a, 0, keepdims=True) for a in expo])
             expo = [a.astype(BF16) for a in expo]
-            if waiting is not None:
-                waiting()
-            waiting = functools.partial(
-                lambda values, put, expo, m, l: put(values(expo), m, l), values, put, expo, m, l
-            )
-            scores = following
-        waiting()
+            if len(waiting) == behind:
+                put_first, values_first, *first = waiting.pop(0)
+                put_first(values_first(first[0]), first[1], first[2])
+            waiting.append((put, values, expo, m, l))
+        for put, values, expo, m, l in waiting:
+            put(values(expo), m, l)
 
     def keep(o_ref, m_ref, l_ref, at, p, o, m, l):
         o_ref[at + (pl.ds(2 * p * HD, HD),)] = o[:HD, :blk]

time: 18.3 us -> 18.3 us (level)
  no operation moved by 1% of the time
where the time goes in v8:
time: 18.3 us; the launch traced here: 18.2 us
  Pallas kernels  16.8 us (92%)
  local copies, waits for them, and re-layouts  0.75 us (4%)
  between operations  0.66 us (4%)
    pallas_call x1, Pallas kernels, local(): pl.pallas_call(functools.partial(kernel, bits, slots, blk), out_shape=plt...  16.8 us
    unnamed x1, local copies, waits for them, and re-layouts  0.75 us

profile of v8, /device:TPU:0, one launch (start us, length us, event | category | flops | bytes accessed | tf_op | source)
XLA Modules:
  0.0 18.2 jit_solution(16281945999189546394)
XLA Ops:
  0.7 16.8 %layer.1 = bf16[384,512]{1,0:T(8,128)(2,1)S(1)} custom-call(bf16[384,512]{1,0:T(8,128)(2,1)} %feat_hbm.1, bf16[3,512,512]{2,1,0:T(8,128)(2,1)} %bitcast.2, bf16[512,512]{1,0:T(8,128)(2,1)} %wo_hbm.1, bf16[512,1024]{1,0:T(8,128)(2,1)} %wu_hbm.1, bf16[1024,512]{1,0:T(8,128)(2,1)} %wd_hbm.1, s32[3,8,128]{2,1,0:T(8,128)} %bitcast.3, s32[3,4]{1,0:T(4,128)} %partner_hbm.1, ...), custom_call_target="tpu_custom_call" | custom-call | flops 5000000000 | bytes 10485760 | tf_op jit(solution)/shard_map/layer/pallas_call | solution.py:286
  17.4 0.7 %copy.10 = bf16[384,512]{1,0:T(8,128)(2,1)} copy(bf16[384,512]{1,0:T(8,128)(2,1)S(1)} %layer.1) | data formatting | bytes 786432
